TPU v7x, 128 devices: a whole 4x4x4 slice. The times are simulated.
128 devices in a mesh: region: 8 (over x_hi, y), acq: 16 (over z, x_lo, core).
Axes of the slice: x: 4 (x_hi: 2, x_lo: 2; x = x_hi * 2 + x_lo), y: 4, z: 4, core: 2. Of those that a mesh axis runs over, the one named last changes fastest.
Arguments:
- scene_lines: bfloat16 [2, 128, 384, 512], P(None, 'acq', 'region'), may hold values from -20 to 20
- assigned_area: int32 [384, 1], P('region'), may hold values from 0 to 7; in each aligned block of 48 rows (0 to 47, 48 to 95, ...) at most 8 rows name the same one
Outputs:
- coherence: float32 [2, 128, 128, 4096], P(None, 'acq', None, 'region')
Inputs may be any that keep to these rules, and one draw needn't show every extreme that they name: `assigned_area`: in every aligned block of 48 rows (the rows of one burst file) no region is named by more than 8 rows, a bound that some block reaches.
All inputs are finite; a program needn't handle non-finite values.
Results may differ from a plain program's by a relative error of at most 0.007.
Values may be sent and summed in bfloat16 or wider, within the bound.
A program may use at most 256 MiB of HBM per device.

v0:
```python
import jax
import jax.numpy as jnp
from jax import lax
from jax.sharding import PartitionSpec as P

LINES_EACH_AREA = 8


def shifted(value, axis, by):
    devices = lax.axis_size(axis)
    return lax.ppermute(value, axis, [(i, (i + by) % devices) for i in range(devices)])


def row_table(rows):
    index = jnp.arange(4, dtype=jnp.float32)
    taper = jnp.exp(-0.5 * ((index - 1.5) / 1.5) ** 2)
    taper = taper / jnp.sum(taper)
    rpos = jnp.arange(rows, dtype=jnp.int32)
    wins = jnp.arange(rows // 4, dtype=jnp.int32)
    values = taper[rpos % 4]
    return jnp.where(wins[:, None] == (rpos // 4)[None, :], values[None, :], jnp.float32(0.0))


def col_table(cols):
    index = jnp.arange(16, dtype=jnp.float32)
    taper = jnp.exp(-0.5 * ((index - 7.5) / 5.0) ** 2)
    taper = taper / jnp.sum(taper)
    cpos = jnp.arange(cols, dtype=jnp.int32)
    wins = jnp.arange(cols // 16, dtype=jnp.int32)
    values = taper[cpos % 16]
    table = jnp.where((cpos // 16)[:, None] == wins[None, :], values[:, None], jnp.float32(0.0))
    return table.astype(jnp.bfloat16)


def multilook(x, row_weights, col_weights):
    cols = jnp.einsum("...rc,cl->...rl", x, col_weights, preferred_element_type=jnp.float32)
    rowed = jnp.einsum("sr,...rl->...sl", row_weights, cols, precision=lax.Precision.HIGHEST)
    return rowed.reshape(rowed.shape[:-2] + (rowed.shape[-2] * rowed.shape[-1],))


def rank_rows(aimed_area, regions, blocks):
    overall_tally = aimed_area.shape[0]
    membership_grid = (aimed_area[:, None] == jnp.arange(regions, dtype=jnp.int32)[None, :]).astype(
        jnp.int32
    )
    tallied_lines = jnp.cumsum(
        membership_grid.reshape(blocks, overall_tally // blocks, regions), axis=1
    ).reshape(overall_tally, regions)
    return jnp.sum(membership_grid * tallied_lines, axis=1) - 1


def local(scene_lines, assigned_area):
    regions = lax.axis_size("region")
    aimed_area = assigned_area[:, 0]
    worker_ordinal = rank_rows(aimed_area, regions, 1)
    slot = aimed_area * LINES_EACH_AREA + worker_ordinal
    picking_grid = (
        jnp.arange(regions * LINES_EACH_AREA, dtype=jnp.int32)[:, None] == slot[None, :]
    ).astype(jnp.bfloat16)
    outgoing = jnp.einsum(
        "bz,ghzj->ghbj", picking_grid, scene_lines, preferred_element_type=jnp.float32
    ).astype(jnp.bfloat16)
    area_bands = lax.all_to_all(outgoing, "region", split_axis=2, concat_axis=2, tiled=True)
    acq_count = lax.axis_size("acq")
    mine = lax.axis_index("acq")
    tile_acqs = area_bands.shape[1]
    row_weights = row_table(area_bands.shape[2])
    col_weights = col_table(area_bands.shape[3])
    real = area_bands[0].astype(jnp.float32)
    imag = area_bands[1].astype(jnp.float32)
    power = (real * real + imag * imag).astype(jnp.bfloat16)
    own_intensity = multilook(power, row_weights, col_weights)
    looks = own_intensity.shape[1]

    def pair_block(visitor, visitor_intensity):
        qr = visitor[0].astype(jnp.float32)
        qi = visitor[1].astype(jnp.float32)
        pre = real[:, None] * qr[None] + imag[:, None] * qi[None]
        pim = imag[:, None] * qr[None] - real[:, None] * qi[None]
        product = jnp.stack([pre, pim]).astype(jnp.bfloat16)
        looked = multilook(product, row_weights, col_weights)
        denom = jnp.sqrt(own_intensity[:, None, :] * visitor_intensity[None, :, :] + 1e-06)
        return looked / denom[None]

    def place(result, block_values, source):
        start = source * tile_acqs
        zero = jnp.int32(0)
        return lax.dynamic_update_slice(result, block_values, (zero, zero, start, zero))

    result = jnp.zeros((2, tile_acqs, tile_acqs * acq_count, looks), jnp.float32)
    result = place(result, pair_block(area_bands, own_intensity), mine)

    def turn(step, carry):
        visitor, visitor_intensity, result = carry
        visitor, visitor_intensity = (
            shifted(visitor, "acq", 1),
            shifted(visitor_intensity.astype(jnp.bfloat16), "acq", 1).astype(
                visitor_intensity.dtype
            ),
        )
        source = (mine - step) % acq_count
        result = place(result, pair_block(visitor, visitor_intensity), source)
        return (visitor, visitor_intensity, result)

    carried = lax.fori_loop(1, acq_count, turn, (area_bands, own_intensity, result))
    result = carried[2]
    return result


def solution(mesh):
    placed = (P(None, "acq", "region", None), P("region", None))
    return jax.shard_map(
        local, mesh=mesh, in_specs=placed, out_specs=P(None, "acq", None, "region"), check_vma=False
    )
```

profile of v0, /device:TPU:4, one launch (start us, length us, event | category | flops | bytes accessed | tf_op | source)
XLA Modules:
  0.0 561.0 jit_solution(16566685680087772229)
XLA Ops:
  4.5 7.4 %all-to-all-start = ((bf16[2,8,64,512]{3,1,0,2:T(8,128)(2,1)}), bf16[2,8,64,512]{3,1,0,2:T(8,128)(2,1)S(1)}, u32[]{:S(2)}, u32[]{:S(2)}) async-start(bf16[2,8,64,512]{3,1,0,2:T(8,128)(2,1)} %copy.3), calls=%async_computation | async-start | bytes 2097152 | tf_op jit(solution)/shard_map/all_to_all | solution.py:63
  18.7 4.3 compare_select_fusion.1
  23.7 5.5 select_select_fusion
  41.4 8.2 %convolution_bitcast_fusion.1 = f32[2,8,8,16,32]{4,3,2,1,0:T(8,128)S(1)} fusion(f32[2,8,8,64,32]{3,4,2,1,0:T(8,128)S(1)} %fusion.23, f32[64]{0:T(128)S(1)} %fusion.57, s32[64]{0:T(128)S(1)} %and_select_fusion.2), kind=kOutput, calls=%fused_computation.38 | convolution fusion | flops 50333696 | bytes 1311232 | tf_op jit(solution)/shard_map/sr,...rl->...sl/dot_general | solution.py:37
  52.7 508.1 %while.21 = (s32[]{:T(128)}, bf16[2,8,64,512]{3,2,1,0:T(8,128)(2,1)S(1)}, f32[8,512]{1,0:T(8,128)S(1)}, f32[2,8,128,512]{3,2,1,0:T(8,128)}, f32[8,64,512]{2,1,0:...) while((s32[]{:T(128)}, ...), condition=%wide.wide.region_5.6_spmd.clone, body=%wide.wide.region_4.5_spmd.clone.sunk | while | flops 340436992 | bytes 34197416 | solution.py:105
  54.1 15.1 %collective-permute-done.1 = bf16[8,512]{1,0:T(8,128)(2,1)S(1)} collective-permute-done((bf16[8,512]{1,0:T(8,128)(2,1)S(1)}, bf16[8,512]{1,0:T(8,128)(2,1)S(1)}, u32[]{:S(2)}, u32[]{:S(2)}) %collective-permute-start.1) | collective-permute-done | bytes 8224 | tf_op jit(solution)/shard_map/while/body/eval_jaxpr/ppermute | solution.py:11
  77.0 8.2 %convolution_bitcast_fusion.5 = f32[2,8,8,16,32]{4,3,2,1,0:T(8,128)S(1)} fusion(f32[2,8,8,64,32]{3,4,2,1,0:T(8,128)S(1)} %fusion.88, f32[64]{0:T(128)S(1)} %get-tuple-element.532, s32[64]{0:T(128)S(1)} %get-tuple-element.531), kind=kOutput, calls=%fused_computation.8.clone.clone.1 | convolution fusion | flops 50333696 | bytes 1311232 | tf_op jit(solution)/shard_map/while/body/eval_jaxpr/sr,...rl->...sl/dot_general | solution.py:37
  86.8 16.3 %collective-permute-done.1 = bf16[8,512]{1,0:T(8,128)(2,1)S(1)} collective-permute-done((bf16[8,512]{1,0:T(8,128)(2,1)S(1)}, bf16[8,512]{1,0:T(8,128)(2,1)S(1)}, u32[]{:S(2)}, u32[]{:S(2)}) %collective-permute-start.1) | collective-permute-done | bytes 8224 | tf_op jit(solution)/shard_map/while/body/eval_jaxpr/ppermute | solution.py:11
  107.0 4.0 fusion.88
  110.9 8.2 %convolution_bitcast_fusion.5 = f32[2,8,8,16,32]{4,3,2,1,0:T(8,128)S(1)} fusion(f32[2,8,8,64,32]{3,4,2,1,0:T(8,128)S(1)} %fusion.88, f32[64]{0:T(128)S(1)} %get-tuple-element.532, s32[64]{0:T(128)S(1)} %get-tuple-element.531), kind=kOutput, calls=%fused_computation.8.clone.clone.1 | convolution fusion | flops 50333696 | bytes 1311232 | tf_op jit(solution)/shard_map/while/body/eval_jaxpr/sr,...rl->...sl/dot_general | solution.py:37
  120.6 16.3 %collective-permute-done.1 = bf16[8,512]{1,0:T(8,128)(2,1)S(1)} collective-permute-done((bf16[8,512]{1,0:T(8,128)(2,1)S(1)}, bf16[8,512]{1,0:T(8,128)(2,1)S(1)}, u32[]{:S(2)}, u32[]{:S(2)}) %collective-permute-start.1) | collective-permute-done | bytes 8224 | tf_op jit(solution)/shard_map/while/body/eval_jaxpr/ppermute | solution.py:11
  140.8 4.0 fusion.88
  144.8 8.2 %convolution_bitcast_fusion.5 = f32[2,8,8,16,32]{4,3,2,1,0:T(8,128)S(1)} fusion(f32[2,8,8,64,32]{3,4,2,1,0:T(8,128)S(1)} %fusion.88, f32[64]{0:T(128)S(1)} %get-tuple-element.532, s32[64]{0:T(128)S(1)} %get-tuple-element.531), kind=kOutput, calls=%fused_computation.8.clone.clone.1 | convolution fusion | flops 50333696 | bytes 1311232 | tf_op jit(solution)/shard_map/while/body/eval_jaxpr/sr,...rl->...sl/dot_general | solution.py:37
  154.5 16.3 %collective-permute-done.1 = bf16[8,512]{1,0:T(8,128)(2,1)S(1)} collective-permute-done((bf16[8,512]{1,0:T(8,128)(2,1)S(1)}, bf16[8,512]{1,0:T(8,128)(2,1)S(1)}, u32[]{:S(2)}, u32[]{:S(2)}) %collective-permute-start.1) | collective-permute-done | bytes 8224 | tf_op jit(solution)/shard_map/while/body/eval_jaxpr/ppermute | solution.py:11
  174.7 4.0 fusion.88
  178.7 8.2 %convolution_bitcast_fusion.5 = f32[2,8,8,16,32]{4,3,2,1,0:T(8,128)S(1)} fusion(f32[2,8,8,64,32]{3,4,2,1,0:T(8,128)S(1)} %fusion.88, f32[64]{0:T(128)S(1)} %get-tuple-element.532, s32[64]{0:T(128)S(1)} %get-tuple-element.531), kind=kOutput, calls=%fused_computation.8.clone.clone.1 | convolution fusion | flops 50333696 | bytes 1311232 | tf_op jit(solution)/shard_map/while/body/eval_jaxpr/sr,...rl->...sl/dot_general | solution.py:37
  188.4 16.3 %collective-permute-done.1 = bf16[8,512]{1,0:T(8,128)(2,1)S(1)} collective-permute-done((bf16[8,512]{1,0:T(8,128)(2,1)S(1)}, bf16[8,512]{1,0:T(8,128)(2,1)S(1)}, u32[]{:S(2)}, u32[]{:S(2)}) %collective-permute-start.1) | collective-permute-done | bytes 8224 | tf_op jit(solution)/shard_map/while/body/eval_jaxpr/ppermute | solution.py:11
  208.6 4.0 fusion.88
  212.6 8.2 %convolution_bitcast_fusion.5 = f32[2,8,8,16,32]{4,3,2,1,0:T(8,128)S(1)} fusion(f32[2,8,8,64,32]{3,4,2,1,0:T(8,128)S(1)} %fusion.88, f32[64]{0:T(128)S(1)} %get-tuple-element.532, s32[64]{0:T(128)S(1)} %get-tuple-element.531), kind=kOutput, calls=%fused_computation.8.clone.clone.1 | convolution fusion | flops 50333696 | bytes 1311232 | tf_op jit(solution)/shard_map/while/body/eval_jaxpr/sr,...rl->...sl/dot_general | solution.py:37
  222.3 16.3 %collective-permute-done.1 = bf16[8,512]{1,0:T(8,128)(2,1)S(1)} collective-permute-done((bf16[8,512]{1,0:T(8,128)(2,1)S(1)}, bf16[8,512]{1,0:T(8,128)(2,1)S(1)}, u32[]{:S(2)}, u32[]{:S(2)}) %collective-permute-start.1) | collective-permute-done | bytes 8224 | tf_op jit(solution)/shard_map/while/body/eval_jaxpr/ppermute | solution.py:11
  242.5 4.0 fusion.88
  246.5 8.2 %convolution_bitcast_fusion.5 = f32[2,8,8,16,32]{4,3,2,1,0:T(8,128)S(1)} fusion(f32[2,8,8,64,32]{3,4,2,1,0:T(8,128)S(1)} %fusion.88, f32[64]{0:T(128)S(1)} %get-tuple-element.532, s32[64]{0:T(128)S(1)} %get-tuple-element.531), kind=kOutput, calls=%fused_computation.8.clone.clone.1 | convolution fusion | flops 50333696 | bytes 1311232 | tf_op jit(solution)/shard_map/while/body/eval_jaxpr/sr,...rl->...sl/dot_general | solution.py:37
  256.2 16.3 %collective-permute-done.1 = bf16[8,512]{1,0:T(8,128)(2,1)S(1)} collective-permute-done((bf16[8,512]{1,0:T(8,128)(2,1)S(1)}, bf16[8,512]{1,0:T(8,128)(2,1)S(1)}, u32[]{:S(2)}, u32[]{:S(2)}) %collective-permute-start.1) | collective-permute-done | bytes 8224 | tf_op jit(solution)/shard_map/while/body/eval_jaxpr/ppermute | solution.py:11
  276.4 4.0 fusion.88
  280.3 8.2 %convolution_bitcast_fusion.5 = f32[2,8,8,16,32]{4,3,2,1,0:T(8,128)S(1)} fusion(f32[2,8,8,64,32]{3,4,2,1,0:T(8,128)S(1)} %fusion.88, f32[64]{0:T(128)S(1)} %get-tuple-element.532, s32[64]{0:T(128)S(1)} %get-tuple-element.531), kind=kOutput, calls=%fused_computation.8.clone.clone.1 | convolution fusion | flops 50333696 | bytes 1311232 | tf_op jit(solution)/shard_map/while/body/eval_jaxpr/sr,...rl->...sl/dot_general | solution.py:37
  290.0 16.3 %collective-permute-done.1 = bf16[8,512]{1,0:T(8,128)(2,1)S(1)} collective-permute-done((bf16[8,512]{1,0:T(8,128)(2,1)S(1)}, bf16[8,512]{1,0:T(8,128)(2,1)S(1)}, u32[]{:S(2)}, u32[]{:S(2)}) %collective-permute-start.1) | collective-permute-done | bytes 8224 | tf_op jit(solution)/shard_map/while/body/eval_jaxpr/ppermute | solution.py:11
  310.2 4.0 fusion.88
  314.2 8.2 %convolution_bitcast_fusion.5 = f32[2,8,8,16,32]{4,3,2,1,0:T(8,128)S(1)} fusion(f32[2,8,8,64,32]{3,4,2,1,0:T(8,128)S(1)} %fusion.88, f32[64]{0:T(128)S(1)} %get-tuple-element.532, s32[64]{0:T(128)S(1)} %get-tuple-element.531), kind=kOutput, calls=%fused_computation.8.clone.clone.1 | convolution fusion | flops 50333696 | bytes 1311232 | tf_op jit(solution)/shard_map/while/body/eval_jaxpr/sr,...rl->...sl/dot_general | solution.py:37
  323.9 16.3 %collective-permute-done.1 = bf16[8,512]{1,0:T(8,128)(2,1)S(1)} collective-permute-done((bf16[8,512]{1,0:T(8,128)(2,1)S(1)}, bf16[8,512]{1,0:T(8,128)(2,1)S(1)}, u32[]{:S(2)}, u32[]{:S(2)}) %collective-permute-start.1) | collective-permute-done | bytes 8224 | tf_op jit(solution)/shard_map/while/body/eval_jaxpr/ppermute | solution.py:11
  344.1 4.0 fusion.88
  348.1 8.2 %convolution_bitcast_fusion.5 = f32[2,8,8,16,32]{4,3,2,1,0:T(8,128)S(1)} fusion(f32[2,8,8,64,32]{3,4,2,1,0:T(8,128)S(1)} %fusion.88, f32[64]{0:T(128)S(1)} %get-tuple-element.532, s32[64]{0:T(128)S(1)} %get-tuple-element.531), kind=kOutput, calls=%fused_computation.8.clone.clone.1 | convolution fusion | flops 50333696 | bytes 1311232 | tf_op jit(solution)/shard_map/while/body/eval_jaxpr/sr,...rl->...sl/dot_general | solution.py:37
  357.8 16.3 %collective-permute-done.1 = bf16[8,512]{1,0:T(8,128)(2,1)S(1)} collective-permute-done((bf16[8,512]{1,0:T(8,128)(2,1)S(1)}, bf16[8,512]{1,0:T(8,128)(2,1)S(1)}, u32[]{:S(2)}, u32[]{:S(2)}) %collective-permute-start.1) | collective-permute-done | bytes 8224 | tf_op jit(solution)/shard_map/while/body/eval_jaxpr/ppermute | solution.py:11
  378.0 4.0 fusion.88
  382.0 8.2 %convolution_bitcast_fusion.5 = f32[2,8,8,16,32]{4,3,2,1,0:T(8,128)S(1)} fusion(f32[2,8,8,64,32]{3,4,2,1,0:T(8,128)S(1)} %fusion.88, f32[64]{0:T(128)S(1)} %get-tuple-element.532, s32[64]{0:T(128)S(1)} %get-tuple-element.531), kind=kOutput, calls=%fused_computation.8.clone.clone.1 | convolution fusion | flops 50333696 | bytes 1311232 | tf_op jit(solution)/shard_map/while/body/eval_jaxpr/sr,...rl->...sl/dot_general | solution.py:37
  391.7 16.3 %collective-permute-done.1 = bf16[8,512]{1,0:T(8,128)(2,1)S(1)} collective-permute-done((bf16[8,512]{1,0:T(8,128)(2,1)S(1)}, bf16[8,512]{1,0:T(8,128)(2,1)S(1)}, u32[]{:S(2)}, u32[]{:S(2)}) %collective-permute-start.1) | collective-permute-done | bytes 8224 | tf_op jit(solution)/shard_map/while/body/eval_jaxpr/ppermute | solution.py:11
  411.9 4.0 fusion.88
  415.9 8.2 %convolution_bitcast_fusion.5 = f32[2,8,8,16,32]{4,3,2,1,0:T(8,128)S(1)} fusion(f32[2,8,8,64,32]{3,4,2,1,0:T(8,128)S(1)} %fusion.88, f32[64]{0:T(128)S(1)} %get-tuple-element.532, s32[64]{0:T(128)S(1)} %get-tuple-element.531), kind=kOutput, calls=%fused_computation.8.clone.clone.1 | convolution fusion | flops 50333696 | bytes 1311232 | tf_op jit(solution)/shard_map/while/body/eval_jaxpr/sr,...rl->...sl/dot_general | solution.py:37
  425.6 16.3 %collective-permute-done.1 = bf16[8,512]{1,0:T(8,128)(2,1)S(1)} collective-permute-done((bf16[8,512]{1,0:T(8,128)(2,1)S(1)}, bf16[8,512]{1,0:T(8,128)(2,1)S(1)}, u32[]{:S(2)}, u32[]{:S(2)}) %collective-permute-start.1) | collective-permute-done | bytes 8224 | tf_op jit(solution)/shard_map/while/body/eval_jaxpr/ppermute | solution.py:11
  445.8 4.0 fusion.88
  449.7 8.2 %convolution_bitcast_fusion.5 = f32[2,8,8,16,32]{4,3,2,1,0:T(8,128)S(1)} fusion(f32[2,8,8,64,32]{3,4,2,1,0:T(8,128)S(1)} %fusion.88, f32[64]{0:T(128)S(1)} %get-tuple-element.532, s32[64]{0:T(128)S(1)} %get-tuple-element.531), kind=kOutput, calls=%fused_computation.8.clone.clone.1 | convolution fusion | flops 50333696 | bytes 1311232 | tf_op jit(solution)/shard_map/while/body/eval_jaxpr/sr,...rl->...sl/dot_general | solution.py:37
  459.4 16.3 %collective-permute-done.1 = bf16[8,512]{1,0:T(8,128)(2,1)S(1)} collective-permute-done((bf16[8,512]{1,0:T(8,128)(2,1)S(1)}, bf16[8,512]{1,0:T(8,128)(2,1)S(1)}, u32[]{:S(2)}, u32[]{:S(2)}) %collective-permute-start.1) | collective-permute-done | bytes 8224 | tf_op jit(solution)/shard_map/while/body/eval_jaxpr/ppermute | solution.py:11
  483.6 8.2 %convolution_bitcast_fusion.5 = f32[2,8,8,16,32]{4,3,2,1,0:T(8,128)S(1)} fusion(f32[2,8,8,64,32]{3,4,2,1,0:T(8,128)S(1)} %fusion.88, f32[64]{0:T(128)S(1)} %get-tuple-element.532, s32[64]{0:T(128)S(1)} %get-tuple-element.531), kind=kOutput, calls=%fused_computation.8.clone.clone.1 | convolution fusion | flops 50333696 | bytes 1311232 | tf_op jit(solution)/shard_map/while/body/eval_jaxpr/sr,...rl->...sl/dot_general | solution.py:37
  493.3 16.3 %collective-permute-done.1 = bf16[8,512]{1,0:T(8,128)(2,1)S(1)} collective-permute-done((bf16[8,512]{1,0:T(8,128)(2,1)S(1)}, bf16[8,512]{1,0:T(8,128)(2,1)S(1)}, u32[]{:S(2)}, u32[]{:S(2)}) %collective-permute-start.1) | collective-permute-done | bytes 8224 | tf_op jit(solution)/shard_map/while/body/eval_jaxpr/ppermute | solution.py:11
  513.5 4.0 fusion.88
  517.5 8.2 %convolution_bitcast_fusion.5 = f32[2,8,8,16,32]{4,3,2,1,0:T(8,128)S(1)} fusion(f32[2,8,8,64,32]{3,4,2,1,0:T(8,128)S(1)} %fusion.88, f32[64]{0:T(128)S(1)} %get-tuple-element.532, s32[64]{0:T(128)S(1)} %get-tuple-element.531), kind=kOutput, calls=%fused_computation.8.clone.clone.1 | convolution fusion | flops 50333696 | bytes 1311232 | tf_op jit(solution)/shard_map/while/body/eval_jaxpr/sr,...rl->...sl/dot_general | solution.py:37
  527.2 16.3 %collective-permute-done.1 = bf16[8,512]{1,0:T(8,128)(2,1)S(1)} collective-permute-done((bf16[8,512]{1,0:T(8,128)(2,1)S(1)}, bf16[8,512]{1,0:T(8,128)(2,1)S(1)}, u32[]{:S(2)}, u32[]{:S(2)}) %collective-permute-start.1) | collective-permute-done | bytes 8224 | tf_op jit(solution)/shard_map/while/body/eval_jaxpr/ppermute | solution.py:11
  547.4 4.0 fusion.88
  551.4 8.2 %convolution_bitcast_fusion.5 = f32[2,8,8,16,32]{4,3,2,1,0:T(8,128)S(1)} fusion(f32[2,8,8,64,32]{3,4,2,1,0:T(8,128)S(1)} %fusion.88, f32[64]{0:T(128)S(1)} %get-tuple-element.532, s32[64]{0:T(128)S(1)} %get-tuple-element.531), kind=kOutput, calls=%fused_computation.8.clone.clone.1 | convolution fusion | flops 50333696 | bytes 1311232 | tf_op jit(solution)/shard_map/while/body/eval_jaxpr/sr,...rl->...sl/dot_general | solution.py:37
  (213 shorter events, 115.5 us)
Async XLA Ops:
  0.0 2.4 copy-start
  4.5 24.8 %all-to-all-start = ((bf16[2,8,64,512]{3,1,0,2:T(8,128)(2,1)}), bf16[2,8,64,512]{3,1,0,2:T(8,128)(2,1)S(1)}, u32[]{:S(2)}, u32[]{:S(2)}) async-start(bf16[2,8,64,512]{3,1,0,2:T(8,128)(2,1)} %copy.3), calls=%async_computation | async-start | bytes 2097152 | tf_op jit(solution)/shard_map/all_to_all | solution.py:63
  29.9 7.6 %copy-start.2 = (f32[8,16,32]{2,1,0:T(8,128)}, f32[8,16,32]{2,1,0:T(8,128)S(1)}, u32[]{:S(2)}) copy-start(f32[8,16,32]{2,1,0:T(8,128)S(1)} %convolution_bitcast_fusion.2) | copy-start | bytes 49156
  50.7 2.0 copy-start.1
  52.7 16.5 %collective-permute-start = (bf16[2,8,64,512]{3,2,1,0:T(8,128)(2,1)S(1)}, bf16[2,8,64,512]{3,2,1,0:T(8,128)(2,1)S(1)}, u32[]{:S(2)}, u32[]{:S(2)}) collective-permute-start(bf16[2,8,64,512]{3,2,1,0:T(8,128)(2,1)S(1)} %get-tuple-element.503), channel_id=1, source_target_pairs={{0,1},{1,2},{2,3},{3,4},{4,5},{5,6},{6,7},{7,8},{8,9},{9,10},{10,1... | collective-permute-start | bytes 3145736 | tf_op jit(solution)/shard_map/while/body/eval_jaxpr/ppermute | solution.py:11
  52.8 16.4 %collective-permute-start.1 = (bf16[8,512]{1,0:T(8,128)(2,1)S(1)}, bf16[8,512]{1,0:T(8,128)(2,1)S(1)}, u32[]{:S(2)}, u32[]{:S(2)}) collective-permute-start(bf16[8,512]{1,0:T(8,128)(2,1)S(1)} %convert_element_type.129), channel_id=1, source_target_pairs={{0,1},{1,2},{2,3},{3,4},{4,5},{5,6},{6,7},{7,8},{8,9},{9,10},{10,1... | collective-permute-start | bytes 24584 | tf_op jit(solution)/shard_map/while/body/eval_jaxpr/ppermute | solution.py:11
  86.6 16.5 %collective-permute-start = (bf16[2,8,64,512]{3,2,1,0:T(8,128)(2,1)S(1)}, bf16[2,8,64,512]{3,2,1,0:T(8,128)(2,1)S(1)}, u32[]{:S(2)}, u32[]{:S(2)}) collective-permute-start(bf16[2,8,64,512]{3,2,1,0:T(8,128)(2,1)S(1)} %get-tuple-element.503), channel_id=1, source_target_pairs={{0,1},{1,2},{2,3},{3,4},{4,5},{5,6},{6,7},{7,8},{8,9},{9,10},{10,1... | collective-permute-start | bytes 3145736 | tf_op jit(solution)/shard_map/while/body/eval_jaxpr/ppermute | solution.py:11
  86.7 16.4 %collective-permute-start.1 = (bf16[8,512]{1,0:T(8,128)(2,1)S(1)}, bf16[8,512]{1,0:T(8,128)(2,1)S(1)}, u32[]{:S(2)}, u32[]{:S(2)}) collective-permute-start(bf16[8,512]{1,0:T(8,128)(2,1)S(1)} %convert_element_type.129), channel_id=1, source_target_pairs={{0,1},{1,2},{2,3},{3,4},{4,5},{5,6},{6,7},{7,8},{8,9},{9,10},{10,1... | collective-permute-start | bytes 24584 | tf_op jit(solution)/shard_map/while/body/eval_jaxpr/ppermute | solution.py:11
  120.4 16.5 %collective-permute-start = (bf16[2,8,64,512]{3,2,1,0:T(8,128)(2,1)S(1)}, bf16[2,8,64,512]{3,2,1,0:T(8,128)(2,1)S(1)}, u32[]{:S(2)}, u32[]{:S(2)}) collective-permute-start(bf16[2,8,64,512]{3,2,1,0:T(8,128)(2,1)S(1)} %get-tuple-element.503), channel_id=1, source_target_pairs={{0,1},{1,2},{2,3},{3,4},{4,5},{5,6},{6,7},{7,8},{8,9},{9,10},{10,1... | collective-permute-start | bytes 3145736 | tf_op jit(solution)/shard_map/while/body/eval_jaxpr/ppermute | solution.py:11
  120.5 16.4 %collective-permute-start.1 = (bf16[8,512]{1,0:T(8,128)(2,1)S(1)}, bf16[8,512]{1,0:T(8,128)(2,1)S(1)}, u32[]{:S(2)}, u32[]{:S(2)}) collective-permute-start(bf16[8,512]{1,0:T(8,128)(2,1)S(1)} %convert_element_type.129), channel_id=1, source_target_pairs={{0,1},{1,2},{2,3},{3,4},{4,5},{5,6},{6,7},{7,8},{8,9},{9,10},{10,1... | collective-permute-start | bytes 24584 | tf_op jit(solution)/shard_map/while/body/eval_jaxpr/ppermute | solution.py:11
  154.3 16.5 %collective-permute-start = (bf16[2,8,64,512]{3,2,1,0:T(8,128)(2,1)S(1)}, bf16[2,8,64,512]{3,2,1,0:T(8,128)(2,1)S(1)}, u32[]{:S(2)}, u32[]{:S(2)}) collective-permute-start(bf16[2,8,64,512]{3,2,1,0:T(8,128)(2,1)S(1)} %get-tuple-element.503), channel_id=1, source_target_pairs={{0,1},{1,2},{2,3},{3,4},{4,5},{5,6},{6,7},{7,8},{8,9},{9,10},{10,1... | collective-permute-start | bytes 3145736 | tf_op jit(solution)/shard_map/while/body/eval_jaxpr/ppermute | solution.py:11
  154.4 16.4 %collective-permute-start.1 = (bf16[8,512]{1,0:T(8,128)(2,1)S(1)}, bf16[8,512]{1,0:T(8,128)(2,1)S(1)}, u32[]{:S(2)}, u32[]{:S(2)}) collective-permute-start(bf16[8,512]{1,0:T(8,128)(2,1)S(1)} %convert_element_type.129), channel_id=1, source_target_pairs={{0,1},{1,2},{2,3},{3,4},{4,5},{5,6},{6,7},{7,8},{8,9},{9,10},{10,1... | collective-permute-start | bytes 24584 | tf_op jit(solution)/shard_map/while/body/eval_jaxpr/ppermute | solution.py:11
  188.2 16.5 %collective-permute-start = (bf16[2,8,64,512]{3,2,1,0:T(8,128)(2,1)S(1)}, bf16[2,8,64,512]{3,2,1,0:T(8,128)(2,1)S(1)}, u32[]{:S(2)}, u32[]{:S(2)}) collective-permute-start(bf16[2,8,64,512]{3,2,1,0:T(8,128)(2,1)S(1)} %get-tuple-element.503), channel_id=1, source_target_pairs={{0,1},{1,2},{2,3},{3,4},{4,5},{5,6},{6,7},{7,8},{8,9},{9,10},{10,1... | collective-permute-start | bytes 3145736 | tf_op jit(solution)/shard_map/while/body/eval_jaxpr/ppermute | solution.py:11
  188.3 16.4 %collective-permute-start.1 = (bf16[8,512]{1,0:T(8,128)(2,1)S(1)}, bf16[8,512]{1,0:T(8,128)(2,1)S(1)}, u32[]{:S(2)}, u32[]{:S(2)}) collective-permute-start(bf16[8,512]{1,0:T(8,128)(2,1)S(1)} %convert_element_type.129), channel_id=1, source_target_pairs={{0,1},{1,2},{2,3},{3,4},{4,5},{5,6},{6,7},{7,8},{8,9},{9,10},{10,1... | collective-permute-start | bytes 24584 | tf_op jit(solution)/shard_map/while/body/eval_jaxpr/ppermute | solution.py:11
  222.1 16.5 %collective-permute-start = (bf16[2,8,64,512]{3,2,1,0:T(8,128)(2,1)S(1)}, bf16[2,8,64,512]{3,2,1,0:T(8,128)(2,1)S(1)}, u32[]{:S(2)}, u32[]{:S(2)}) collective-permute-start(bf16[2,8,64,512]{3,2,1,0:T(8,128)(2,1)S(1)} %get-tuple-element.503), channel_id=1, source_target_pairs={{0,1},{1,2},{2,3},{3,4},{4,5},{5,6},{6,7},{7,8},{8,9},{9,10},{10,1... | collective-permute-start | bytes 3145736 | tf_op jit(solution)/shard_map/while/body/eval_jaxpr/ppermute | solution.py:11
  222.2 16.4 %collective-permute-start.1 = (bf16[8,512]{1,0:T(8,128)(2,1)S(1)}, bf16[8,512]{1,0:T(8,128)(2,1)S(1)}, u32[]{:S(2)}, u32[]{:S(2)}) collective-permute-start(bf16[8,512]{1,0:T(8,128)(2,1)S(1)} %convert_element_type.129), channel_id=1, source_target_pairs={{0,1},{1,2},{2,3},{3,4},{4,5},{5,6},{6,7},{7,8},{8,9},{9,10},{10,1... | collective-permute-start | bytes 24584 | tf_op jit(solution)/shard_map/while/body/eval_jaxpr/ppermute | solution.py:11
  256.0 16.5 %collective-permute-start = (bf16[2,8,64,512]{3,2,1,0:T(8,128)(2,1)S(1)}, bf16[2,8,64,512]{3,2,1,0:T(8,128)(2,1)S(1)}, u32[]{:S(2)}, u32[]{:S(2)}) collective-permute-start(bf16[2,8,64,512]{3,2,1,0:T(8,128)(2,1)S(1)} %get-tuple-element.503), channel_id=1, source_target_pairs={{0,1},{1,2},{2,3},{3,4},{4,5},{5,6},{6,7},{7,8},{8,9},{9,10},{10,1... | collective-permute-start | bytes 3145736 | tf_op jit(solution)/shard_map/while/body/eval_jaxpr/ppermute | solution.py:11
  256.1 16.4 %collective-permute-start.1 = (bf16[8,512]{1,0:T(8,128)(2,1)S(1)}, bf16[8,512]{1,0:T(8,128)(2,1)S(1)}, u32[]{:S(2)}, u32[]{:S(2)}) collective-permute-start(bf16[8,512]{1,0:T(8,128)(2,1)S(1)} %convert_element_type.129), channel_id=1, source_target_pairs={{0,1},{1,2},{2,3},{3,4},{4,5},{5,6},{6,7},{7,8},{8,9},{9,10},{10,1... | collective-permute-start | bytes 24584 | tf_op jit(solution)/shard_map/while/body/eval_jaxpr/ppermute | solution.py:11
  289.8 16.5 %collective-permute-start = (bf16[2,8,64,512]{3,2,1,0:T(8,128)(2,1)S(1)}, bf16[2,8,64,512]{3,2,1,0:T(8,128)(2,1)S(1)}, u32[]{:S(2)}, u32[]{:S(2)}) collective-permute-start(bf16[2,8,64,512]{3,2,1,0:T(8,128)(2,1)S(1)} %get-tuple-element.503), channel_id=1, source_target_pairs={{0,1},{1,2},{2,3},{3,4},{4,5},{5,6},{6,7},{7,8},{8,9},{9,10},{10,1... | collective-permute-start | bytes 3145736 | tf_op jit(solution)/shard_map/while/body/eval_jaxpr/ppermute | solution.py:11
  289.9 16.4 %collective-permute-start.1 = (bf16[8,512]{1,0:T(8,128)(2,1)S(1)}, bf16[8,512]{1,0:T(8,128)(2,1)S(1)}, u32[]{:S(2)}, u32[]{:S(2)}) collective-permute-start(bf16[8,512]{1,0:T(8,128)(2,1)S(1)} %convert_element_type.129), channel_id=1, source_target_pairs={{0,1},{1,2},{2,3},{3,4},{4,5},{5,6},{6,7},{7,8},{8,9},{9,10},{10,1... | collective-permute-start | bytes 24584 | tf_op jit(solution)/shard_map/while/body/eval_jaxpr/ppermute | solution.py:11
  323.7 16.5 %collective-permute-start = (bf16[2,8,64,512]{3,2,1,0:T(8,128)(2,1)S(1)}, bf16[2,8,64,512]{3,2,1,0:T(8,128)(2,1)S(1)}, u32[]{:S(2)}, u32[]{:S(2)}) collective-permute-start(bf16[2,8,64,512]{3,2,1,0:T(8,128)(2,1)S(1)} %get-tuple-element.503), channel_id=1, source_target_pairs={{0,1},{1,2},{2,3},{3,4},{4,5},{5,6},{6,7},{7,8},{8,9},{9,10},{10,1... | collective-permute-start | bytes 3145736 | tf_op jit(solution)/shard_map/while/body/eval_jaxpr/ppermute | solution.py:11
  323.8 16.4 %collective-permute-start.1 = (bf16[8,512]{1,0:T(8,128)(2,1)S(1)}, bf16[8,512]{1,0:T(8,128)(2,1)S(1)}, u32[]{:S(2)}, u32[]{:S(2)}) collective-permute-start(bf16[8,512]{1,0:T(8,128)(2,1)S(1)} %convert_element_type.129), channel_id=1, source_target_pairs={{0,1},{1,2},{2,3},{3,4},{4,5},{5,6},{6,7},{7,8},{8,9},{9,10},{10,1... | collective-permute-start | bytes 24584 | tf_op jit(solution)/shard_map/while/body/eval_jaxpr/ppermute | solution.py:11
  357.6 16.5 %collective-permute-start = (bf16[2,8,64,512]{3,2,1,0:T(8,128)(2,1)S(1)}, bf16[2,8,64,512]{3,2,1,0:T(8,128)(2,1)S(1)}, u32[]{:S(2)}, u32[]{:S(2)}) collective-permute-start(bf16[2,8,64,512]{3,2,1,0:T(8,128)(2,1)S(1)} %get-tuple-element.503), channel_id=1, source_target_pairs={{0,1},{1,2},{2,3},{3,4},{4,5},{5,6},{6,7},{7,8},{8,9},{9,10},{10,1... | collective-permute-start | bytes 3145736 | tf_op jit(solution)/shard_map/while/body/eval_jaxpr/ppermute | solution.py:11
  357.7 16.4 %collective-permute-start.1 = (bf16[8,512]{1,0:T(8,128)(2,1)S(1)}, bf16[8,512]{1,0:T(8,128)(2,1)S(1)}, u32[]{:S(2)}, u32[]{:S(2)}) collective-permute-start(bf16[8,512]{1,0:T(8,128)(2,1)S(1)} %convert_element_type.129), channel_id=1, source_target_pairs={{0,1},{1,2},{2,3},{3,4},{4,5},{5,6},{6,7},{7,8},{8,9},{9,10},{10,1... | collective-permute-start | bytes 24584 | tf_op jit(solution)/shard_map/while/body/eval_jaxpr/ppermute | solution.py:11
  391.5 16.5 %collective-permute-start = (bf16[2,8,64,512]{3,2,1,0:T(8,128)(2,1)S(1)}, bf16[2,8,64,512]{3,2,1,0:T(8,128)(2,1)S(1)}, u32[]{:S(2)}, u32[]{:S(2)}) collective-permute-start(bf16[2,8,64,512]{3,2,1,0:T(8,128)(2,1)S(1)} %get-tuple-element.503), channel_id=1, source_target_pairs={{0,1},{1,2},{2,3},{3,4},{4,5},{5,6},{6,7},{7,8},{8,9},{9,10},{10,1... | collective-permute-start | bytes 3145736 | tf_op jit(solution)/shard_map/while/body/eval_jaxpr/ppermute | solution.py:11
  391.6 16.4 %collective-permute-start.1 = (bf16[8,512]{1,0:T(8,128)(2,1)S(1)}, bf16[8,512]{1,0:T(8,128)(2,1)S(1)}, u32[]{:S(2)}, u32[]{:S(2)}) collective-permute-start(bf16[8,512]{1,0:T(8,128)(2,1)S(1)} %convert_element_type.129), channel_id=1, source_target_pairs={{0,1},{1,2},{2,3},{3,4},{4,5},{5,6},{6,7},{7,8},{8,9},{9,10},{10,1... | collective-permute-start | bytes 24584 | tf_op jit(solution)/shard_map/while/body/eval_jaxpr/ppermute | solution.py:11
  425.4 16.5 %collective-permute-start = (bf16[2,8,64,512]{3,2,1,0:T(8,128)(2,1)S(1)}, bf16[2,8,64,512]{3,2,1,0:T(8,128)(2,1)S(1)}, u32[]{:S(2)}, u32[]{:S(2)}) collective-permute-start(bf16[2,8,64,512]{3,2,1,0:T(8,128)(2,1)S(1)} %get-tuple-element.503), channel_id=1, source_target_pairs={{0,1},{1,2},{2,3},{3,4},{4,5},{5,6},{6,7},{7,8},{8,9},{9,10},{10,1... | collective-permute-start | bytes 3145736 | tf_op jit(solution)/shard_map/while/body/eval_jaxpr/ppermute | solution.py:11
  425.5 16.4 %collective-permute-start.1 = (bf16[8,512]{1,0:T(8,128)(2,1)S(1)}, bf16[8,512]{1,0:T(8,128)(2,1)S(1)}, u32[]{:S(2)}, u32[]{:S(2)}) collective-permute-start(bf16[8,512]{1,0:T(8,128)(2,1)S(1)} %convert_element_type.129), channel_id=1, source_target_pairs={{0,1},{1,2},{2,3},{3,4},{4,5},{5,6},{6,7},{7,8},{8,9},{9,10},{10,1... | collective-permute-start | bytes 24584 | tf_op jit(solution)/shard_map/while/body/eval_jaxpr/ppermute | solution.py:11
  459.2 16.5 %collective-permute-start = (bf16[2,8,64,512]{3,2,1,0:T(8,128)(2,1)S(1)}, bf16[2,8,64,512]{3,2,1,0:T(8,128)(2,1)S(1)}, u32[]{:S(2)}, u32[]{:S(2)}) collective-permute-start(bf16[2,8,64,512]{3,2,1,0:T(8,128)(2,1)S(1)} %get-tuple-element.503), channel_id=1, source_target_pairs={{0,1},{1,2},{2,3},{3,4},{4,5},{5,6},{6,7},{7,8},{8,9},{9,10},{10,1... | collective-permute-start | bytes 3145736 | tf_op jit(solution)/shard_map/while/body/eval_jaxpr/ppermute | solution.py:11
  459.3 16.4 %collective-permute-start.1 = (bf16[8,512]{1,0:T(8,128)(2,1)S(1)}, bf16[8,512]{1,0:T(8,128)(2,1)S(1)}, u32[]{:S(2)}, u32[]{:S(2)}) collective-permute-start(bf16[8,512]{1,0:T(8,128)(2,1)S(1)} %convert_element_type.129), channel_id=1, source_target_pairs={{0,1},{1,2},{2,3},{3,4},{4,5},{5,6},{6,7},{7,8},{8,9},{9,10},{10,1... | collective-permute-start | bytes 24584 | tf_op jit(solution)/shard_map/while/body/eval_jaxpr/ppermute | solution.py:11
  493.1 16.5 %collective-permute-start = (bf16[2,8,64,512]{3,2,1,0:T(8,128)(2,1)S(1)}, bf16[2,8,64,512]{3,2,1,0:T(8,128)(2,1)S(1)}, u32[]{:S(2)}, u32[]{:S(2)}) collective-permute-start(bf16[2,8,64,512]{3,2,1,0:T(8,128)(2,1)S(1)} %get-tuple-element.503), channel_id=1, source_target_pairs={{0,1},{1,2},{2,3},{3,4},{4,5},{5,6},{6,7},{7,8},{8,9},{9,10},{10,1... | collective-permute-start | bytes 3145736 | tf_op jit(solution)/shard_map/while/body/eval_jaxpr/ppermute | solution.py:11
  493.2 16.4 %collective-permute-start.1 = (bf16[8,512]{1,0:T(8,128)(2,1)S(1)}, bf16[8,512]{1,0:T(8,128)(2,1)S(1)}, u32[]{:S(2)}, u32[]{:S(2)}) collective-permute-start(bf16[8,512]{1,0:T(8,128)(2,1)S(1)} %convert_element_type.129), channel_id=1, source_target_pairs={{0,1},{1,2},{2,3},{3,4},{4,5},{5,6},{6,7},{7,8},{8,9},{9,10},{10,1... | collective-permute-start | bytes 24584 | tf_op jit(solution)/shard_map/while/body/eval_jaxpr/ppermute | solution.py:11
  527.0 16.5 %collective-permute-start = (bf16[2,8,64,512]{3,2,1,0:T(8,128)(2,1)S(1)}, bf16[2,8,64,512]{3,2,1,0:T(8,128)(2,1)S(1)}, u32[]{:S(2)}, u32[]{:S(2)}) collective-permute-start(bf16[2,8,64,512]{3,2,1,0:T(8,128)(2,1)S(1)} %get-tuple-element.503), channel_id=1, source_target_pairs={{0,1},{1,2},{2,3},{3,4},{4,5},{5,6},{6,7},{7,8},{8,9},{9,10},{10,1... | collective-permute-start | bytes 3145736 | tf_op jit(solution)/shard_map/while/body/eval_jaxpr/ppermute | solution.py:11
  527.1 16.4 %collective-permute-start.1 = (bf16[8,512]{1,0:T(8,128)(2,1)S(1)}, bf16[8,512]{1,0:T(8,128)(2,1)S(1)}, u32[]{:S(2)}, u32[]{:S(2)}) collective-permute-start(bf16[8,512]{1,0:T(8,128)(2,1)S(1)} %convert_element_type.129), channel_id=1, source_target_pairs={{0,1},{1,2},{2,3},{3,4},{4,5},{5,6},{6,7},{7,8},{8,9},{9,10},{10,1... | collective-permute-start | bytes 24584 | tf_op jit(solution)/shard_map/while/body/eval_jaxpr/ppermute | solution.py:11
where the time goes:
time: 562 us; the launch traced here: 561 us
  waiting for transfers between devices  243 us (43%)
  matrix products  196 us (35%)
  other arithmetic  91.2 us (16%)
  local copies, waits for them, and re-layouts  17.7 us (3%)
  starting transfers between devices  10.8 us (2%)
    ppermute x30, waiting for transfers between devices, shifted(): lax.ppermute(value, axis, [(i, (i + by) % devices) for i in range(devices)])  243 us
    dot_general x17, matrix products, multilook(): jnp.einsum('sr,...rl->...sl', row_weights, cols, precision=lax.Precision....  132 us
    dot_general x17, matrix products, multilook(): jnp.einsum('...rc,cl->...rl', x, col_weights, preferred_element_type=jnp....  63.9 us
    another operation x16, other arithmetic  57.2 us
  transfers between devices with their start and end apart: 31, of which 15 were waited for; matrix products, arithmetic and copies ran while one was open for 3% of the time, Pallas kernels for 0%

commit v1 on v0

v1 whole, which is shorter than its diff:
```python
import functools

import jax
import jax.numpy as jnp
from jax import lax
from jax.experimental import pallas as pl
from jax.experimental.pallas import tpu as pltpu
from jax.sharding import Mesh
from jax.sharding import PartitionSpec as P

F32 = jnp.float32
BF16 = jnp.bfloat16
NT = (((1,), (1,)), ((), ()))
GROUPS = ((0, 1), (2, 3))


def weight_tables():
    index = jnp.arange(4, dtype=F32)
    rows = jnp.exp(-0.5 * ((index - 1.5) / 1.5) ** 2)
    rows = rows / jnp.sum(rows)
    index = jnp.arange(16, dtype=F32)
    cols = jnp.exp(-0.5 * ((index - 7.5) / 5.0) ** 2)
    cols = (cols / jnp.sum(cols)).astype(BF16).astype(F32)
    c = jnp.arange(128, dtype=jnp.int32)
    mask = jnp.where(jnp.arange(8)[:, None] == (c // 16)[None, :], cols[c % 16][None, :], 0.0)
    return rows, mask.astype(F32)


def strip_sources(area):
    b = jnp.arange(48, dtype=jnp.int32)
    same = (area[:, None] == area[None, :]) & (b[None, :] < b[:, None])
    slot = area * 8 + jnp.sum(same.astype(jnp.int32), axis=1)
    match = (jnp.arange(64, dtype=jnp.int32)[:, None] == slot[None, :]).astype(jnp.int32)
    src = jnp.sum(match * b[None, :], axis=1)
    return src, jnp.sum(match, axis=1).astype(F32)


def build_own(src, fill, rows, mask, z0, lhs):
    def window(w, _):
        for r in range(4):
            s = w * 4 + r
            table = mask[...] * (rows[r] * fill[s])
            own = z0[src[s], pl.ds(0, 64), :].astype(F32)
            wide = own[:, None, :] * table[None, :, :]
            lhs[w, :, r * 128 : (r + 1) * 128] = wide.reshape(512, 128).astype(BF16)
        return 0

    lax.fori_loop(0, 16, window, 0)


def swap_parts(x):
    lane = lax.broadcasted_iota(jnp.int32, x.shape, x.ndim - 1)
    up = pltpu.roll(x, 120, axis=x.ndim - 1)
    down = pltpu.roll(x, 8, axis=x.ndim - 1)
    return jnp.where((lane // 8) % 2 == 0, up, down)


def window_coherence(w, src, fill, rows, mask, z, lhs, own_power, first):
    parts, powers = [], []
    for r in range(4):
        s = w * 4 + r
        row = z[src[s]]
        parts.append(row)
        wide = row.astype(F32)
        powers.append((wide * wide * (rows[r] * fill[s])).astype(BF16))
    data = jnp.concatenate(parts, axis=1)
    power = jnp.concatenate(powers, axis=1)
    looks = jnp.concatenate([mask[...].astype(BF16)] * 4, axis=1)
    halves = lax.dot_general(looks, power, NT, preferred_element_type=F32)
    lane = lax.broadcasted_iota(jnp.int32, (8, 128), 1)
    intensity = halves + swap_parts(halves)
    if first:
        for i in range(32):
            at = (i // 8) * 16 + i % 8
            own_power[w, i] = jnp.broadcast_to(intensity[:, at : at + 1], (8, 128))
    full = lax.dot_general(lhs[w], data, NT, preferred_element_type=F32)
    full = full.reshape(4, 2, 64, 128)
    sign = jnp.where((lane // 8) % 2 == 0, 1.0, -1.0).astype(F32)
    re_rows = full[:, 0].reshape(32, 8, 128)
    im_rows = full[:, 1].reshape(256, 128)
    total = swap_parts(im_rows).reshape(32, 8, 128) + sign[None] * re_rows
    scale = lax.rsqrt(own_power[w] * intensity[None] + 1e-6)
    return total * scale


def pairs_kernel(src, fill, rows, mask, z, out, lhs, own_power):
    build_own(src, fill, rows, mask, z.at[0], lhs)
    for g in range(2):

        def region(o, _):
            both = [
                window_coherence(o * 2 + h, src, fill, rows, mask, z.at[g], lhs, own_power, g == 0)
                for h in range(2)
            ]
            both = jnp.stack(both, axis=1).reshape(4, 8, 16, 128)
            out[o, :, g] = both.astype(BF16)
            return 0

        lax.fori_loop(0, 8, region, 0)


def finish_kernel(recv, out):
    z = lax.axis_index("z")
    for g in range(2):
        x = recv[:, g, 0].astype(F32)
        x = x.reshape(8, 4, 2, 8, 128)
        x = jnp.swapaxes(x, 1, 2).reshape(512, 128)
        y = x.T
        for d in range(2):
            at = lax.rem(z + GROUPS[g][d], 4) * 32
            for q in range(4):
                for part in range(2):
                    k = d * 64 + q * 16 + part * 8
                    out[part, 0, pl.ds(pl.multiple_of(at + q * 8, 8), 8), :] = y[k : k + 8]


def local(scene_lines, assigned_area):
    rows, mask = weight_tables()
    src, fill = strip_sources(assigned_area[:, 0])
    staged = scene_lines.reshape(2, 8, 48, 4, 128).transpose(3, 2, 0, 1, 4).reshape(4, 48, 16, 128)
    tiles = lax.all_to_all(staged, ("x_lo", "core"), 0, 0, tiled=True)
    every = lax.all_gather(tiles, "z")
    z = lax.axis_index("z")
    every = jnp.roll(every, -z, axis=0)
    every = every.reshape(2, 8, 48, 16, 128).transpose(0, 2, 1, 3, 4).reshape(2, 48, 128, 128)
    smem = pl.BlockSpec(memory_space=pltpu.SMEM)
    vmem = pl.BlockSpec(memory_space=pltpu.VMEM)
    sent = pl.pallas_call(
        pairs_kernel,
        out_shape=jax.ShapeDtypeStruct((8, 4, 2, 8, 16, 128), BF16),
        in_specs=[smem, smem, smem, vmem, vmem],
        out_specs=vmem,
        scratch_shapes=[pltpu.VMEM((16, 512, 512), BF16), pltpu.VMEM((16, 32, 8, 128), F32)],
        compiler_params=pltpu.CompilerParams(vmem_limit_bytes=48 << 20),
    )(src, fill, rows, mask, every)
    sent = sent.reshape(32, 2, 8, 16, 128)
    got = lax.all_to_all(sent, ("x_hi", "y", "x_lo", "core"), 0, 0, tiled=True)
    return pl.pallas_call(
        finish_kernel,
        grid=(8,),
        out_shape=jax.ShapeDtypeStruct((2, 8, 128, 512), F32),
        in_specs=[pl.BlockSpec((32, 2, 1, 16, 128), lambda i: (0, 0, i, 0, 0))],
        out_specs=pl.BlockSpec((2, 1, 128, 512), lambda i: (0, i, 0, 0)),
        compiler_params=pltpu.CompilerParams(vmem_limit_bytes=32 << 20),
    )(got)


def solution(mesh):
    fine = Mesh(mesh.devices.reshape(2, 4, 4, 2, 2), ("x_hi", "y", "z", "x_lo", "core"))
    region, acq = ("x_hi", "y"), ("z", "x_lo", "core")
    placed = (P(None, acq, region, None), P(region, None))
    return jax.shard_map(
        local, mesh=fine, in_specs=placed, out_specs=P(None, acq, None, region), check_vma=False
    )
```

time: 562 us -> 130 us (0.23)
  the two profiles are of different devices: /device:TPU:4 before, /device:TPU:1 now
where the time goes in v1:
time: 130 us
  blocking collectives  50.5 us (39%)
  waiting for transfers between devices  29.1 us (22%)
  Pallas kernels  16.7 us (13%)
  other arithmetic  15.9 us (12%)
  between operations  13.5 us (10%)
  local copies, waits for them, and re-layouts  3.88 us (3%)
    all_to_all x1, blocking collectives, local(): got = lax.all_to_all(sent, ('x_hi', 'y', 'x_lo', 'core'), 0, 0, tiled=True)  35.3 us
    all_gather x1, waiting for transfers between devices, local(): every = lax.all_gather(tiles, 'z')  29.1 us
    all_to_all x1, blocking collectives, local(): tiles = lax.all_to_all(staged, ('x_lo', 'core'), 0, 0, tiled=True)  15.2 us
    pallas_call x1, Pallas kernels, local(): pl.pallas_call(pairs_kernel, out_shape=jax.ShapeDtypeStruct((8, 4, 2, 8,...  12.6 us
    gather x1, other arithmetic, weight_tables(): cols[c % 16][None, :]  10 us
    pallas_call x1, Pallas kernels, local(): pl.pallas_call(finish_kernel, grid=(8,), out_shape=jax.ShapeDtypeStruct((...  4.09 us
    concatenate x1, other arithmetic, local(): every = jnp.roll(every, -z, axis=0)  3.01 us
  transfers between devices with their start and end apart: 1, of which 1 were waited for; matrix products, arithmetic and copies ran while one was open for 11% of the time, Pallas kernels for 0%

profile of v1, /device:TPU:1, one launch (start us, length us, event | category | flops | bytes accessed | tf_op | source)
XLA Modules:
  0.0 129.6 jit_solution(10119548381663248896)
XLA Ops:
  6.5 0.0 copy-start
  6.5 0.0 all-gather.3.cloned.1.call-start
  6.5 1.8 %reshape.69 = bf16[2,8,48,4,128]{4,3,2,1,0:T(4,128)(2,1)S(1)} reshape(bf16[2,8,48,512]{3,2,1,0:T(8,128)(2,1)} %param.2) | data formatting | bytes 1572864 | tf_op jit(solution)/shard_map/reshape | solution.py:120
  8.3 0.5 copy.10
  8.8 15.2 %all_to_all.10 = bf16[4,48,16,128]{3,2,1,0:T(8,128)(2,1)} all-to-all(bf16[4,48,16,128]{3,2,1,0:T(8,128)(2,1)S(1)} %bitcast.73), channel_id=1, replica_groups=mesh['x_hi'=2,'y'=4,'z'=4,'x_lo'=2,'core'=2] {'x_lo','core'}, dimensions={0} | all-to-all | bytes 1572864 | tf_op jit(solution)/shard_map/all_to_all | solution.py:121
  24.0 0.0 all-gather.3.cloned.1.call-update
  24.0 0.0 copy-done
  24.0 0.2 convert_reduce_fusion.1
  24.2 0.1 convert_reduce_fusion
  24.3 0.6 fusion.4
  25.0 0.6 fusion.5
  25.6 0.6 convert_convert_fusion
  26.2 0.7 broadcast_divide_fusion.rows
  26.9 0.7 fusion.6
  27.6 10.0 %bitcast_select_fusion.8 = f32[128]{0:T(128)S(1)} fusion(f32[]{:T(128)} %bitcast.19, f32[]{:T(128)} %bitcast.20, f32[]{:T(128)} %bitcast.21, f32[]{:T(128)} %bitcast.22, f32[]{:T(128)} %bitcast.23, f32[]{:T(128)} %bitcast.25, f32[]{:T(128)} %bitcast.24, f32[]{:T(128)} %bitcast.2, f32[]{:T(128)} %bitcast.4, f32[]{:T(128)} %bitcast.6, f32[]{:T(128)} %bitcast.8, ...), kind=kLoop, calls=%fused_computation.21 | loop fusion | flops 4992 | bytes 576 | tf_op jit(solution)/shard_map/gather | solution.py:25
  37.7 29.1 %all-gather.3.cloned.1.call-done = bf16[16,48,16,128]{3,2,1,0:T(8,128)(2,1)} async-done(((bf16[4,48,16,128]{3,2,1,0:T(8,128)(2,1)}), bf16[16,48,16,128]{3,2,1,0:T(8,128)(2,1)}) %all-gather.3.cloned.1.call-update) | async-done | bytes 3145744 | tf_op jit(solution)/shard_map/all_gather | solution.py:122
  66.8 3.0 %fusion = bf16[4,4,48,16,128]{4,3,2,1,0:T(8,128)(2,1)S(1)} fusion(s32[]{:T(128)S(6)} %select_n.54, bf16[4,4,48,16,128]{4,3,2,1,0:T(8,128)(2,1)} %bitcast.72), kind=kLoop, calls=%fused_computation.2 | loop fusion | flops 1572864 | bytes 6291460 | tf_op jit(solution)/shard_map/jit(_roll_dynamic)/concatenate | solution.py:124
  69.8 0.9 copy.8
  70.7 12.6 %shard_map.28 = bf16[8,4,2,8,16,128]{5,4,3,2,1,0:T(8,128)(2,1)S(1)} custom-call(s32[64]{0:T(128)S(1)} %get-tuple-element.6.src, f32[64]{0:T(128)S(1)} %convert_element_type.17.fill, f32[4]{0:T(128)S(1)} %broadcast_divide_fusion.rows, f32[8,128]{1,0:T(8,128)S(1)} %fusion.2.mask, bf16[2,48,128,128]{3,2,1,0:T(8,128)(2,1)S(1)} %bitcast.69), custom_call_target="tpu_custom_call" | custom-call | tf_op jit(solution)/shard_map/pallas_call | solution.py:128
  83.3 35.3 %all_to_all.11.recv = bf16[32,2,8,16,128]{4,3,2,1,0:T(8,128)(2,1)S(1)} all-to-all(bf16[32,2,8,16,128]{4,3,2,1,0:T(8,128)(2,1)S(1)} %bitcast.70), channel_id=1, replica_groups=mesh['x_hi'=2,'y'=4,'z'=4,'x_lo'=2,'core'=2] {'x_hi','y','x_lo','core'}, dimensions={0} | all-to-all | bytes 4194304 | tf_op jit(solution)/shard_map/all_to_all | solution.py:137
  118.6 4.1 %shard_map.29 = f32[2,8,128,512]{3,2,1,0:T(8,128)} custom-call(bf16[32,2,8,16,128]{4,3,2,1,0:T(8,128)(2,1)S(1)} %all_to_all.11.recv), custom_call_target="tpu_custom_call" | custom-call | tf_op jit(solution)/shard_map/pallas_call | solution.py:138
  (4 shorter events, 0.0 us)
Async XLA Ops:
  6.5 17.5 %copy-start = (s32[48,1]{0,1:T(1,128)S(1)}, s32[48,1]{0,1:T(1,128)}, u32[]{:S(2)}) copy-start(s32[48,1]{0,1:T(1,128)} %param.3) | copy-start | bytes 580
  6.5 60.2 %all-gather.3.cloned.1.call-start = ((), (), s32[]{:S(2)}) async-start(), calls=%async_computation.2 | async-start | bytes 3932160 | tf_op jit(solution)/shard_map/all_gather | solution.py:122
Sparse Core Ops, SparseCore 0:
  24.1 42.5 all-gather.2

commit v2 on v1

v2 whole, which is shorter than its diff:
```python
import jax
import jax.numpy as jnp
import numpy as np
from jax import lax
from jax.experimental import pallas as pl
from jax.experimental.pallas import tpu as pltpu
from jax.sharding import PartitionSpec as P

F32 = jnp.float32
BF16 = jnp.bfloat16
NT = (((1,), (1,)), ((), ()))
MESH = pl.DeviceIdType.MESH


def taper(length, centre, width):
    index = np.arange(length, dtype=np.float32)
    values = np.exp(np.float32(-0.5) * ((index - np.float32(centre)) / np.float32(width)) ** 2)
    return values / np.sum(values)


ROWS = [float(v) for v in taper(4, 1.5, 1.5)]
COLS = [float(v) for v in taper(16, 7.5, 5.0).astype(jnp.bfloat16).astype(np.float32)]


def look_mask():
    look = lax.broadcasted_iota(jnp.int32, (8, 128), 0)
    col = lax.broadcasted_iota(jnp.int32, (8, 128), 1)
    values = jnp.zeros((8, 128), F32)
    for k in range(16):
        values = jnp.where(col % 16 == k, COLS[k], values)
    return jnp.where(look == col // 16, values, 0.0)


def strip_sources(area):
    b = jnp.arange(48, dtype=jnp.int32)
    same = (area[:, None] == area[None, :]) & (b[None, :] < b[:, None])
    slot = area * 8 + jnp.sum(same.astype(jnp.int32), axis=1)
    match = (jnp.arange(64, dtype=jnp.int32)[:, None] == slot[None, :]).astype(jnp.int32)
    src = jnp.sum(match * b[None, :], axis=1)
    return src, jnp.sum(match, axis=1).astype(F32)


def swap_parts(x):
    lane = lax.broadcasted_iota(jnp.int32, x.shape, x.ndim - 1)
    up = pltpu.roll(x, 120, axis=x.ndim - 1)
    down = pltpu.roll(x, 8, axis=x.ndim - 1)
    return jnp.where((lane // 8) % 2 == 0, up, down)


def build_own(src, fill, mask, z0, lhs):
    def window(w, _):
        for r in range(4):
            s = w * 4 + r
            table = mask * (ROWS[r] * fill[s])
            own = z0[src[s]].astype(F32)
            wide = own[:, None, :] * table[None, :, :]
            lhs[w, :, r * 128 : (r + 1) * 128] = wide.reshape(512, 128).astype(BF16)
        return 0

    lax.fori_loop(0, 16, window, 0)


def window_sums(w, src, fill, looks, z, lhs):
    parts, powers = [], []
    for r in range(4):
        s = w * 4 + r
        row = z[src[s]]
        parts.append(row)
        wide = row.astype(F32)
        powers.append((wide * wide * (ROWS[r] * fill[s])).astype(BF16))
    data = jnp.concatenate(parts, axis=1)
    power = jnp.concatenate(powers, axis=1)
    halves = lax.dot_general(looks, power, NT, preferred_element_type=F32)
    full = lax.dot_general(lhs[w], data, NT, preferred_element_type=F32)
    return full, halves


def coherence(full, halves, own):
    lane = lax.broadcasted_iota(jnp.int32, (8, 128), 1)
    intensity = halves + swap_parts(halves)
    full = full.reshape(4, 2, 64, 128)
    sign = jnp.where((lane // 8) % 2 == 0, 1.0, -1.0).astype(F32)
    re_rows = full[:, 0].reshape(32, 8, 128)
    im_rows = full[:, 1].reshape(256, 128)
    total = swap_parts(im_rows).reshape(32, 8, 128) + sign[None] * re_rows
    return total * lax.rsqrt(own * intensity[None] + 1e-6)


def pairs_kernel(
    src, fill, staged, recv0, recv1, recv2,
    z0, z1, z2, lhs, own_power, res0, res1, res2,
    own_sem, a_send, a_recv, b_send, b_recv, c_send, c_recv,
):
    k = lax.axis_index("region")
    acq = lax.axis_index("acq")
    z = acq // 4
    q = acq % 4
    xl, core = q // 2, q % 2
    right = (k, ((z + 1) % 4) * 4 + q)
    left = (k, ((z + 3) % 4) * 4 + q)

    def tile(j):
        return ((xl + j // 2) % 2) * 2 + (core + j % 2) % 2

    def rows16(start):
        return pl.ds(pl.multiple_of(start, 16), 16)

    barrier = pltpu.get_barrier_semaphore()
    for peer in (left, right):
        pl.semaphore_signal(barrier, inc=1, device_id=peer, device_id_type=MESH)

    def greet(n, _):
        o, p = n // 4, n % 4

        @pl.when(jnp.logical_or(o != k, p != q))
        def _():
            pl.semaphore_signal(barrier, inc=1, device_id=(o, z * 4 + p), device_id_type=MESH)

        return 0

    lax.fori_loop(0, 32, greet, 0)
    pl.semaphore_wait(barrier, 33)

    def remote(from_ref, to_ref, send, recv, peer):
        return pltpu.make_async_remote_copy(
            src_ref=from_ref, dst_ref=to_ref, send_sem=send, recv_sem=recv,
            device_id=peer, device_id_type=MESH,
        )

    a_copies = {}
    for j in (1, 2, 3):
        to = tile(j)
        a_copies[j] = remote(
            staged.at[to], z0.at[:, rows16(q * 16), :], a_send.at[j], a_recv.at[j], (k, z * 4 + to)
        )
        a_copies[j].start()
    own = pltpu.make_async_copy(staged.at[q], z0.at[:, rows16(q * 16), :], own_sem)
    own.start()

    b_copies = {}

    def send_along(j):
        t = tile(j)
        data = staged.at[q] if j == 0 else z0.at[:, rows16(t * 16), :]
        b_copies[j, 0] = remote(
            data, z1.at[:, rows16(t * 16), :], b_send.at[j], b_recv.at[j], right
        )
        b_copies[j, 1] = remote(
            data, z1.at[:, rows16(64 + t * 16), :], b_send.at[4 + j], b_recv.at[4 + j], left
        )
        b_copies[j, 0].start()
        b_copies[j, 1].start()

    send_along(0)
    for j in (1, 2, 3):
        a_copies[j].wait_recv()
        send_along(j)
    own.wait()

    mask = look_mask()
    looks = jnp.concatenate([mask.astype(BF16)] * 4, axis=1)
    build_own(src, fill, mask, z0, lhs)

    def send_results(o, g, res, recv):
        for p in range(4):
            here = jnp.logical_and(o == k, q == p)
            block, land = res.at[o * 4 + p], recv.at[k * 4 + q]

            @pl.when(here)
            def _():
                pltpu.make_async_copy(block, land, c_recv.at[g]).start()

            @pl.when(jnp.logical_not(here))
            def _():
                remote(block, land, c_send.at[g], c_recv.at[g], (o, z * 4 + p)).start()

    lane = lax.broadcasted_iota(jnp.int32, (8, 128), 1)

    def small_group(g, data, res, recv):
        def region(n, _):
            o = (k + n) % 8
            full, halves = [], []
            for h in range(2):
                f, p = window_sums(o * 2 + h, src, fill, looks, data, lhs)
                full.append(f)
                halves.append(p)
            full = jnp.concatenate(full, axis=1)
            halves = jnp.concatenate(halves, axis=1)
            if g == 0:
                intensity = halves + swap_parts(halves)
                for h in range(2):
                    for i in range(32):
                        at = h * 64 + (i // 8) * 16 + i % 8
                        own_power[o * 2 + h, i] = jnp.broadcast_to(
                            intensity[:, at : at + 1], (8, 128)
                        )
            own = jnp.where((lane < 64)[None], own_power[o * 2], own_power[o * 2 + 1])
            both = coherence(full, halves, own).reshape(4, 4, 16, 128)
            res[pl.ds(o * 4, 4)] = both.astype(BF16)
            send_results(o, g, res, recv)
            return 0

        lax.fori_loop(0, 8, region, 0)

    def large_group(g, data, res, recv):
        def region(n, _):
            o = (k + n) % 8
            both = []
            for h in range(2):
                full, halves = window_sums(o * 2 + h, src, fill, looks, data, lhs)
                both.append(coherence(full, halves, own_power[o * 2 + h]))
            both = jnp.stack(both, axis=1).reshape(4, 8, 16, 128)
            res[pl.ds(o * 4, 4)] = both.astype(BF16)
            send_results(o, g, res, recv)
            return 0

        lax.fori_loop(0, 8, region, 0)

    small_group(0, z0, res0, recv0)

    relays = []
    for j in (0, 1):
        b_copies[j, 0].wait_recv()
        t = tile(j)
        relays.append(remote(
            z1.at[:, rows16(t * 16), :], z2.at[:, rows16(t * 16), :],
            b_send.at[8 + j], b_recv.at[8 + j], right,
        ))
        relays[-1].start()
    for j in (2, 3):
        b_copies[j, 1].wait_recv()
        t = tile(j)
        relays.append(remote(
            z1.at[:, rows16(64 + t * 16), :], z2.at[:, rows16(t * 16), :],
            b_send.at[8 + j], b_recv.at[8 + j], left,
        ))
        relays[-1].start()
    for j in (2, 3):
        b_copies[j, 0].wait_recv()
    for j in (0, 1):
        b_copies[j, 1].wait_recv()
    large_group(1, z1, res1, recv1)

    for relay in relays:
        relay.wait_recv()
    small_group(2, z2, res2, recv2)

    for j in (1, 2, 3):
        a_copies[j].wait_send()
    for copy in b_copies.values():
        copy.wait_send()
    for relay in relays:
        relay.wait_send()
    for g, (res, recv) in enumerate(((res0, recv0), (res1, recv1), (res2, recv2))):
        some = pl.ds(0, 31)
        pltpu.make_async_copy(res.at[some], recv.at[some], c_send.at[g]).wait()
        pltpu.make_async_copy(res, recv, c_recv.at[g]).wait()


def finish_kernel(recv0, recv1, recv2, out):
    z = lax.axis_index("acq") // 4
    lane = lax.broadcasted_iota(jnp.int32, (8, 128), 1)
    low = (lane < 64)[None]

    def place(x, offsets, i):
        y = x.reshape(512, 128).T
        for d, offset in enumerate(offsets):
            at = ((z + offset) % 4) * 32
            for q in range(4):
                for part in range(2):
                    n = d * 64 + q * 16 + part * 8
                    out[part, i, pl.ds(pl.multiple_of(at + q * 8, 8), 8), :] = y[n : n + 8]

    for i in range(2):
        a = recv0[:, 0].astype(F32).reshape(32, 2, 8, 128)[:, i]
        b = recv2[:, 0].astype(F32).reshape(32, 2, 8, 128)[:, i]
        turned_a = pltpu.roll(a.reshape(256, 128), 64, axis=1).reshape(32, 8, 128)
        turned_b = pltpu.roll(b.reshape(256, 128), 64, axis=1).reshape(32, 8, 128)
        first = jnp.where(low, a, turned_b).reshape(8, 4, 8, 128)
        second = jnp.where(low, turned_a, b).reshape(8, 4, 8, 128)
        place(jnp.stack([first, second], axis=1), (0, 2), i)
        c = recv1[:, i].astype(F32).reshape(8, 4, 2, 8, 128)
        place(jnp.swapaxes(c, 1, 2), (3, 1), i)


def local(scene_lines, assigned_area):
    src, fill = strip_sources(assigned_area[:, 0])
    staged = scene_lines.reshape(2, 8, 48, 4, 128).transpose(3, 2, 0, 1, 4).reshape(4, 48, 16, 128)
    smem = pl.BlockSpec(memory_space=pltpu.SMEM)
    vmem = pl.BlockSpec(memory_space=pltpu.VMEM)
    hbm = pl.BlockSpec(memory_space=pl.ANY)
    small, large = (32, 4, 16, 128), (32, 8, 16, 128)
    got = pl.pallas_call(
        pairs_kernel,
        out_shape=[jax.ShapeDtypeStruct(shape, BF16) for shape in (small, large, small)],
        in_specs=[smem, smem, vmem],
        out_specs=[hbm, hbm, hbm],
        scratch_shapes=[
            pltpu.VMEM((48, 64, 128), BF16),
            pltpu.VMEM((48, 128, 128), BF16),
            pltpu.VMEM((48, 64, 128), BF16),
            pltpu.VMEM((16, 512, 512), BF16),
            pltpu.VMEM((16, 32, 8, 128), F32),
            pltpu.VMEM(small, BF16),
            pltpu.VMEM(large, BF16),
            pltpu.VMEM(small, BF16),
            pltpu.SemaphoreType.DMA,
            pltpu.SemaphoreType.DMA((4,)),
            pltpu.SemaphoreType.DMA((4,)),
            pltpu.SemaphoreType.DMA((12,)),
            pltpu.SemaphoreType.DMA((12,)),
            pltpu.SemaphoreType.DMA((3,)),
            pltpu.SemaphoreType.DMA((3,)),
        ],
        compiler_params=pltpu.CompilerParams(
            vmem_limit_bytes=40 << 20, collective_id=0, has_side_effects=True
        ),
    )(src, fill, staged)
    return pl.pallas_call(
        finish_kernel,
        grid=(4,),
        out_shape=jax.ShapeDtypeStruct((2, 8, 128, 512), F32),
        in_specs=[
            pl.BlockSpec((32, 1, 16, 128), lambda i: (0, i, 0, 0)),
            pl.BlockSpec((32, 2, 16, 128), lambda i: (0, i, 0, 0)),
            pl.BlockSpec((32, 1, 16, 128), lambda i: (0, i, 0, 0)),
        ],
        out_specs=pl.BlockSpec((2, 2, 128, 512), lambda i: (0, i, 0, 0)),
        compiler_params=pltpu.CompilerParams(vmem_limit_bytes=32 << 20),
    )(*got)


def solution(mesh):
    placed = (P(None, "acq", "region", None), P("region", None))
    return jax.shard_map(
        local, mesh=mesh, in_specs=placed, out_specs=P(None, "acq", None, "region"), check_vma=False
    )
```

time: 130 us -> 58.6 us (0.45)
  blocking collectives: 50.5 us -> 0 us
  Pallas kernels: 16.7 us -> 54.5 us
  waiting for transfers between devices: 29.1 us -> 0 us
  other arithmetic: 15.9 us -> 1.68 us
  between operations: 13.5 us -> 0.03 us
  local copies, waits for them, and re-layouts: 3.88 us -> 2.26 us
    all_to_all x2 -> x0, blocking collectives: 50.5 us -> none  [the longest x1 35.3 us: local(): got = lax.all_to_all(sent, ('x_hi', 'y', 'x_lo', 'core'), 0, 0, tiled=True)]
    pallas_call x2, Pallas kernels: 16.7 us -> 54.5 us  [the longest x1 51.3 us: local(): pl.pallas_call(pairs_kernel, out_shape=[jax.ShapeDtypeStruct(shape, BF16)...]
    all_gather x1 -> x0, waiting for transfers between devices: 29.1 us -> none  [local(): every = lax.all_gather(tiles, 'z')]
    gather x1 -> x0, other arithmetic: 10 us -> none  [weight_tables(): cols[c % 16][None, :]]
    concatenate x1 -> x0, other arithmetic: 3.01 us -> none  [local(): every = jnp.roll(every, -z, axis=0)]
  transfers between devices with their start and end apart: 1 -> 0, of which waited for: 1 -> 0; matrix products, arithmetic and copies ran while one was open for 11% -> 0% of each run, Pallas kernels for 0% -> 0%
where the time goes in v2:
time: 58.6 us; the launch traced here: 58.4 us
  Pallas kernels  54.5 us (93%)
  local copies, waits for them, and re-layouts  2.26 us (4%)
  other arithmetic  1.68 us (3%)
    pallas_call x1, Pallas kernels, local(): pl.pallas_call(pairs_kernel, out_shape=[jax.ShapeDtypeStruct(shape, BF16)...  51.3 us
    pallas_call x1, Pallas kernels, local(): pl.pallas_call(finish_kernel, grid=(4,), out_shape=jax.ShapeDtypeStruct((...  3.12 us
    reshape x2, local copies, waits for them, and re-layouts, local(): scene_lines.reshape(2, 8, 48, 4, 128).transpose(3, 2, 0, 1, 4)  2.26 us

profile of v2, /device:TPU:1, one launch (start us, length us, event | category | flops | bytes accessed | tf_op | source)
XLA Modules:
  0.0 58.4 jit_solution(8026990093546375954)
XLA Ops:
  0.0 0.9 %convert_reduce_fusion.1 = s32[48]{0:T(128)S(1)} fusion(s32[48]{0:T(128)} %bitcast.10), kind=kLoop, calls=%fused_computation.3 | loop fusion | flops 11472 | bytes 384 | tf_op jit(solution)/shard_map/reduce_sum | solution.py:37
  0.9 0.7 %multiply_add_fusion = s32[48]{0:T(128)S(1)} fusion(s32[48]{0:T(128)S(1)} %convert_reduce_fusion.1, s32[48,1]{0,1:T(1,128)} %param.3), kind=kLoop, calls=%fused_computation.7 | loop fusion | flops 96 | bytes 576 | tf_op jit(solution)/shard_map/add | solution.py:37
  1.6 0.1 convert_reduce_fusion
  1.7 1.7 %reshape.15 = bf16[2,8,48,4,128]{4,3,2,1,0:T(4,128)(2,1)S(1)} reshape(bf16[2,8,48,512]{3,2,1,0:T(8,128)(2,1)} %param.2) | data formatting | bytes 1572864 | tf_op jit(solution)/shard_map/reshape | solution.py:288
  3.4 0.5 copy.6
  4.0 51.3 %shard_map.28 = (bf16[32,4,16,128]{3,2,1,0:T(8,128)(2,1)S(1)}, bf16[32,8,16,128]{3,2,1,0:T(8,128)(2,1)S(1)}, bf16[32,4,16,128]{3,2,1,0:T(8,128)(2,1)S(1)}) custom-call(s32[64]{0:T(128)S(1)} %get-tuple-element.12.src, f32[64]{0:T(128)S(1)} %convert_element_type.11.fill, bf16[4,48,16,128]{3,2,1,0:T(8,128)(2,1)S(1)} %bitcast.9), custom_call_target="tpu_custom_call" | custom-call | tf_op jit(solution)/shard_map/pallas_call | solution.py:293
  55.3 3.1 %shard_map.29 = f32[2,8,128,512]{3,2,1,0:T(8,128)} custom-call(bf16[32,4,16,128]{3,2,1,0:T(8,128)(2,1)S(1)} %get-tuple-element.8.recv0, bf16[32,8,16,128]{3,2,1,0:T(8,128)(2,1)S(1)} %get-tuple-element.9.recv1, bf16[32,4,16,128]{3,2,1,0:T(8,128)(2,1)S(1)} %get-tuple-element.10.recv2), custom_call_target="tpu_custom_call" | custom-call | tf_op jit(solution)/shard_map/pallas_call | solution.py:319
  (1 shorter events, 0.0 us)

commit v3 on v2

v3 whole, which is shorter than its diff:
```python
import jax
import jax.numpy as jnp
import numpy as np
from jax import lax
from jax.experimental import pallas as pl
from jax.experimental.pallas import tpu as pltpu
from jax.sharding import PartitionSpec as P

F32 = jnp.float32
BF16 = jnp.bfloat16
NT = (((1,), (1,)), ((), ()))
MESH = pl.DeviceIdType.MESH


def taper(length, centre, width):
    index = np.arange(length, dtype=np.float32)
    values = np.exp(np.float32(-0.5) * ((index - np.float32(centre)) / np.float32(width)) ** 2)
    return values / np.sum(values)


ROWS = [float(v) for v in taper(4, 1.5, 1.5)]
COLS = [float(v) for v in taper(16, 7.5, 5.0).astype(jnp.bfloat16).astype(np.float32)]


def lanes(shape):
    return lax.broadcasted_iota(jnp.int32, shape, len(shape) - 1)


def column_weights():
    col = lanes((8, 128))
    values = jnp.zeros((8, 128), F32)
    for k in range(16):
        values = jnp.where(col % 16 == k, COLS[k], values)
    return values


def swap_parts(x):
    up = pltpu.roll(x, 120, axis=x.ndim - 1)
    down = pltpu.roll(x, 8, axis=x.ndim - 1)
    return jnp.where((lanes(x.shape) // 8) % 2 == 0, up, down)


def sort_rows(area, table):
    slot = lanes((8, 128))
    owner, place = slot // 8, slot % 8
    source = jnp.zeros((8, 128), jnp.int32)
    held = jnp.zeros((8, 128), jnp.int32)
    count = jnp.zeros((8, 128), jnp.int32)
    for b in range(48):
        hit = owner == area[b, 0]
        take = jnp.logical_and(hit, count == place)
        source = jnp.where(take, b, source)
        held = jnp.where(take, 1, held)
        count = count + hit.astype(jnp.int32)
    table[0] = source
    table[1] = held


def stage_columns(scene, wide, staged):
    for part in range(2):
        for a in range(8):
            n = part * 8 + a
            x = scene[part, a].astype(F32)
            for c in range(4):
                wide[c, n * 48 : (n + 1) * 48, :] = x[:, c * 128 : (c + 1) * 128]

    def row(b, _):
        for c in range(4):
            staged[c, b] = wide[c, pl.ds(b, 16, stride=48), :].astype(BF16)
        return 0

    lax.fori_loop(0, 48, row, 0, unroll=4)


def build_own(w, src, weights, z0, lhs):
    look = (lanes((8, 128)) // 16) % 4
    for r in range(4):
        s = w * 4 + r
        table = weights * (ROWS[r] * src[1, 0, s].astype(F32))
        own = z0[src[0, 0, s]].astype(F32).reshape(4, 2, 8, 128)
        tables = [jnp.where(look == l, table, 0.0) for l in range(4)]
        spread = jnp.stack([own * t[None, None] for t in tables], axis=1)
        lhs[w, :, r * 128 : (r + 1) * 128] = spread.reshape(256, 128).astype(BF16)


def window_sums(w, src, weights, z, lhs):
    zero = jnp.zeros((64, 128), BF16)
    low = lanes((64, 128)) < 64
    look = (lanes((8, 128)) // 16) % 4 == lax.broadcasted_iota(jnp.int32, (8, 128), 0)
    data, power, looks = [], [], []
    for r in range(4):
        s = w * 4 + r
        row = z[src[0, 0, s]]
        square = row * row
        data.append(jnp.concatenate([jnp.where(low, row, zero), jnp.where(low, zero, row)], axis=0))
        power.append(
            jnp.concatenate([jnp.where(low, square, zero), jnp.where(low, zero, square)], axis=0)
        )
        table = weights * (ROWS[r] * src[1, 0, s].astype(F32))
        looks.append(jnp.where(look, table, 0.0).astype(BF16))
    data = jnp.concatenate(data, axis=1)
    power = jnp.concatenate(power, axis=1)
    looks = jnp.concatenate(looks, axis=1)
    full = lax.dot_general(lhs[w], data, NT, preferred_element_type=F32)
    halves = lax.dot_general(looks, power, NT, preferred_element_type=F32)
    return full, halves + swap_parts(halves)


def own_intensities(w, intensity, own_power):
    turned = intensity.T
    low = lanes((8, 128)) < 64
    for q in range(4):
        for l in range(4):
            first = jnp.broadcast_to(turned[q * 16 : q * 16 + 8, l : l + 1], (8, 128))
            second = jnp.broadcast_to(turned[64 + q * 16 : 72 + q * 16, l : l + 1], (8, 128))
            own_power[w, q * 4 + l] = jnp.where(low, first, second)


def coherence(full, intensity, own):
    full = full.reshape(16, 2, 8, 128)
    sign = jnp.where((lanes((8, 128)) // 8) % 2 == 0, 1.0, -1.0).astype(F32)
    swapped = swap_parts(full[:, 1].reshape(128, 128)).reshape(16, 8, 128)
    total = swapped + sign[None] * full[:, 0]
    other = jnp.stack([jnp.broadcast_to(intensity[l : l + 1], (8, 128)) for l in range(4)], axis=0)
    product = own.reshape(4, 4, 8, 128) * other[None]
    scale = lax.rsqrt(product + 1e-6)
    return (total.reshape(4, 4, 8, 128) * scale).reshape(4, 2, 16, 128).astype(BF16)


def pairs_kernel(
    area, scene, recv,
    wide, staged, table, src, z0, z1, z2, z3, lhs, own_power, res,
    local_sem, a_send, a_recv, b_send, b_recv, c_send, c_recv,
):
    zs = (z0, z1, z2, z3)
    k = lax.axis_index("region")
    acq = lax.axis_index("acq")
    z = acq // 4
    q = acq % 4
    xl, core = q // 2, q % 2
    right = (k, ((z + 1) % 4) * 4 + q)
    left = (k, ((z + 3) % 4) * 4 + q)

    def tile(j):
        return ((xl + j // 2) % 2) * 2 + (core + j % 2) % 2

    def rows16(start):
        return pl.ds(pl.multiple_of(start, 16), 16)

    barrier = pltpu.get_barrier_semaphore()
    for peer in (left, right):
        pl.semaphore_signal(barrier, inc=1, device_id=peer, device_id_type=MESH)

    def greet(n, _):
        o, p = n // 4, n % 4

        @pl.when(jnp.logical_or(o != k, p != q))
        def _():
            pl.semaphore_signal(barrier, inc=1, device_id=(o, z * 4 + p), device_id_type=MESH)

        return 0

    lax.fori_loop(0, 32, greet, 0)

    sort_rows(area, table)
    sorted_rows = pltpu.make_async_copy(table, src, local_sem.at[0])
    sorted_rows.start()
    stage_columns(scene, wide, staged)
    pl.semaphore_wait(barrier, 33)

    def remote(from_ref, to_ref, send, recv, peer):
        return pltpu.make_async_remote_copy(
            src_ref=from_ref, dst_ref=to_ref, send_sem=send, recv_sem=recv,
            device_id=peer, device_id_type=MESH,
        )

    a_copies = {}
    for j in (2, 3, 1):
        to = tile(j)
        a_copies[j] = remote(
            staged.at[to], zs[0].at[:, rows16(q * 16), :], a_send.at[j], a_recv.at[j],
            (k, z * 4 + to),
        )
        a_copies[j].start()

    def near(j, side):
        return zs[1 + j // 2].at[:, rows16(side * 32 + ((core + j) % 2) * 16), :]

    b_copies = {}

    def send_along(j):
        data = staged.at[q] if j == 0 else zs[0].at[:, rows16(tile(j) * 16), :]
        for side, peer in ((0, right), (1, left)):
            n = side * 4 + j
            b_copies[j, side] = remote(data, near(j, side), b_send.at[n], b_recv.at[n], peer)
            b_copies[j, side].start()

    send_along(0)
    own = pltpu.make_async_copy(staged.at[q], zs[0].at[:, rows16(q * 16), :], local_sem.at[1])
    own.start()
    for j in (1, 2, 3):
        a_copies[j].wait_recv()
        send_along(j)
    own.wait()
    sorted_rows.wait()

    weights = column_weights()

    def send_results(o, g):
        for p in range(4):
            here = jnp.logical_and(o == k, q == p)
            block, land = res.at[g, o * 4 + p], recv.at[g, k * 4 + q]

            @pl.when(here)
            def _():
                pltpu.make_async_copy(block, land, c_recv.at[g]).start()

            @pl.when(jnp.logical_not(here))
            def _():
                remote(block, land, c_send.at[g], c_recv.at[g], (o, z * 4 + p)).start()

    def group(g):
        def step(n, _):
            regions = (
                ((k // 4 + n) % 2) * 4 + (k + n + 1) % 4,
                ((k // 4 + n + 1) % 2) * 4 + (k + n + 3) % 4,
            )
            if g == 0:
                for o in regions:
                    for h in range(2):
                        build_own(o * 2 + h, src, weights, zs[0], lhs)
            sums = [
                window_sums(o * 2 + h, src, weights, zs[g], lhs)
                for o in regions
                for h in range(2)
            ]
            if g == 0:
                for m, o in enumerate(regions):
                    for h in range(2):
                        own_intensities(o * 2 + h, sums[m * 2 + h][1], own_power)
            for m, o in enumerate(regions):
                for h in range(2):
                    full, intensity = sums[m * 2 + h]
                    block = coherence(full, intensity, own_power[o * 2 + h])
                    res[g, pl.ds(o * 4, 4), h * 2 : h * 2 + 2] = block
                send_results(o, g)
            return 0

        lax.fori_loop(0, 4, step, 0)

    group(0)
    for j in (0, 1):
        for side in range(2):
            b_copies[j, side].wait_recv()
    group(1)

    relays = []

    def relay(j):
        side, peer = ((0, right), (0, right), (1, left), (1, left))[j]
        n = 8 + j
        relays.append(remote(
            near(j, side), zs[3].at[:, rows16(tile(j) * 16), :], b_send.at[n], b_recv.at[n], peer
        ))
        relays[-1].start()

    relay(0)
    relay(1)
    for j in (2, 3):
        b_copies[j, 1].wait_recv()
        relay(j)
    for j in (2, 3):
        b_copies[j, 0].wait_recv()
    group(2)
    for copy in relays:
        copy.wait_recv()
    group(3)

    for copy in list(a_copies.values()) + list(b_copies.values()) + relays:
        copy.wait_send()
    for g in range(4):
        some = pl.ds(0, 31)
        pltpu.make_async_copy(res.at[g, some], recv.at[g, some], c_send.at[g]).wait()
        pltpu.make_async_copy(res.at[g], recv.at[g], c_recv.at[g]).wait()


def finish_kernel(recv, out, mixed):
    z = lax.axis_index("acq") // 4
    low = lanes((8, 128)) < 64

    def arrange(x, y, m):
        def half_turn(v):
            return pltpu.roll(v.reshape(512, 128), 64, axis=1).reshape(v.shape)

        first = jnp.where(low, x, half_turn(y))
        second = jnp.where(low, half_turn(x), y)
        both = jnp.stack([first, second], axis=3)
        both = both.transpose(0, 2, 1, 3, 4, 5, 6)
        mixed[m] = both.reshape(1024, 128)

    parts = [recv[g].astype(F32).reshape(2, 4, 2, 4, 8, 128) for g in range(4)]
    arrange(parts[0], parts[3], 0)
    near = jnp.concatenate([parts[1][:, 0:2], parts[2][:, 2:4]], axis=1)
    far = jnp.concatenate([parts[2][:, 0:2], parts[1][:, 2:4]], axis=1)
    arrange(near, far, 1)
    for i in range(8):
        for m in range(2):
            y = mixed[m, pl.ds(i, 128, stride=8), :].T
            for n in range(8):
                if m == 0:
                    offset, t = (n // 4) * 2, n % 4
                else:
                    offset, t = 3 + (n // 2) % 2 * 2, (n // 4) * 2 + n % 2
                at = ((z + offset) % 4) * 32 + t * 8
                for part in range(2):
                    lane = n * 16 + part * 8
                    out[part, i, pl.ds(pl.multiple_of(at, 8), 8), :] = y[lane : lane + 8]


def local(scene_lines, assigned_area):
    smem = pl.BlockSpec(memory_space=pltpu.SMEM)
    vmem = pl.BlockSpec(memory_space=pltpu.VMEM)
    hbm = pl.BlockSpec(memory_space=pl.ANY)
    blocks = (4, 32, 4, 16, 128)
    got = pl.pallas_call(
        pairs_kernel,
        out_shape=jax.ShapeDtypeStruct(blocks, BF16),
        in_specs=[smem, vmem],
        out_specs=hbm,
        scratch_shapes=[
            pltpu.VMEM((4, 768, 128), F32),
            pltpu.VMEM((4, 48, 16, 128), BF16),
            pltpu.VMEM((2, 8, 128), jnp.int32),
            pltpu.SMEM((2, 8, 128), jnp.int32),
            pltpu.VMEM((48, 64, 128), BF16),
            pltpu.VMEM((48, 64, 128), BF16),
            pltpu.VMEM((48, 64, 128), BF16),
            pltpu.VMEM((48, 64, 128), BF16),
            pltpu.VMEM((16, 256, 512), BF16),
            pltpu.VMEM((16, 16, 8, 128), F32),
            pltpu.VMEM(blocks, BF16),
            pltpu.SemaphoreType.DMA((2,)),
            pltpu.SemaphoreType.DMA((4,)),
            pltpu.SemaphoreType.DMA((4,)),
            pltpu.SemaphoreType.DMA((12,)),
            pltpu.SemaphoreType.DMA((12,)),
            pltpu.SemaphoreType.DMA((4,)),
            pltpu.SemaphoreType.DMA((4,)),
        ],
        compiler_params=pltpu.CompilerParams(
            vmem_limit_bytes=40 << 20, collective_id=0, has_side_effects=True
        ),
    )(assigned_area, scene_lines)
    return pl.pallas_call(
        finish_kernel,
        grid=(4,),
        out_shape=jax.ShapeDtypeStruct((2, 8, 128, 512), F32),
        in_specs=[pl.BlockSpec((4, 8, 4, 16, 128), lambda n: (0, n, 0, 0, 0))],
        out_specs=pl.BlockSpec((2, 8, 128, 128), lambda n: (0, 0, 0, n)),
        scratch_shapes=[pltpu.VMEM((2, 1024, 128), F32)],
        compiler_params=pltpu.CompilerParams(vmem_limit_bytes=32 << 20),
    )(got)


def solution(mesh):
    placed = (P(None, "acq", "region", None), P("region", None))
    return jax.shard_map(
        local, mesh=mesh, in_specs=placed, out_specs=P(None, "acq", None, "region"), check_vma=False
    )
```

time: 58.6 us -> 56.4 us (0.962)
  other arithmetic: 1.68 us -> 0 us
    reshape x2 -> x0, local copies, waits for them, and re-layouts: 2.26 us -> none  [local(): scene_lines.reshape(2, 8, 48, 4, 128).transpose(3, 2, 0, 1, 4)]
    unnamed x0 -> x3, local copies, waits for them, and re-layouts: none -> 1.87 us
    reduce_sum x2 -> x0, other arithmetic: 1 us -> none  [the longest x1 0.91 us: strip_sources(): slot = area * 8 + jnp.sum(same.astype(jnp.int32), axis=1)]
    pallas_call x1, Pallas kernels: 51.3 us -> 50.7 us  [local(): pl.pallas_call(pairs_kernel, out_shape=jax.ShapeDtypeStruct(blocks, BF16)...]
    add x1 -> x0, other arithmetic: 0.67 us -> none  [strip_sources(): slot = area * 8 + jnp.sum(same.astype(jnp.int32), axis=1)]
    pallas_call x1, Pallas kernels: 3.12 us -> 3.72 us  [local(): pl.pallas_call(finish_kernel, grid=(4,), out_shape=jax.ShapeDtypeStruct((...]
where the time goes in v3:
time: 56.4 us; the launch traced here: 56.3 us
  Pallas kernels  54.4 us (96%)
  local copies, waits for them, and re-layouts  1.87 us (3%)
    pallas_call x1, Pallas kernels, local(): pl.pallas_call(pairs_kernel, out_shape=jax.ShapeDtypeStruct(blocks, BF16)...  50.7 us
    pallas_call x1, Pallas kernels, local(): pl.pallas_call(finish_kernel, grid=(4,), out_shape=jax.ShapeDtypeStruct((...  3.72 us
    unnamed x3, local copies, waits for them, and re-layouts  1.87 us

profile of v3, /device:TPU:1, one launch (start us, length us, event | category | flops | bytes accessed | tf_op | source)
XLA Modules:
  0.0 56.3 jit_solution(2611714122739881683)
XLA Ops:
  0.0 0.7 %copy.3.area = s32[48,1]{1,0:T(8,128)S(1)} copy(s32[48,1]{0,1:T(1,128)} %param.3) | data formatting | bytes 384 | tf_op args[1]
  0.7 0.0 copy-start
  0.7 1.1 %copy-done = bf16[2,8,48,512]{3,2,1,0:T(8,128)(2,1)S(1)} copy-done((bf16[2,8,48,512]{3,2,1,0:T(8,128)(2,1)S(1)}, bf16[2,8,48,512]{3,2,1,0:T(8,128)(2,1)}, u32[]{:S(2)}) %copy-start) | copy-done | bytes 786456
  1.9 50.7 %shard_map.28.recv = bf16[4,32,4,16,128]{4,3,2,1,0:T(8,128)(2,1)S(1)} custom-call(s32[48,1]{1,0:T(8,128)S(1)} %copy.3.area, bf16[2,8,48,512]{3,2,1,0:T(8,128)(2,1)S(1)} %copy-done), custom_call_target="tpu_custom_call" | custom-call | tf_op jit(solution)/shard_map/pallas_call | solution.py:325
  52.5 3.7 %shard_map.29 = f32[2,8,128,512]{3,2,1,0:T(8,128)} custom-call(bf16[4,32,4,16,128]{4,3,2,1,0:T(8,128)(2,1)S(1)} %shard_map.28.recv), custom_call_target="tpu_custom_call" | custom-call | tf_op jit(solution)/shard_map/pallas_call | solution.py:354
Async XLA Ops:
  0.7 1.1 %copy-start = (bf16[2,8,48,512]{3,2,1,0:T(8,128)(2,1)S(1)}, bf16[2,8,48,512]{3,2,1,0:T(8,128)(2,1)}, u32[]{:S(2)}) copy-start(bf16[2,8,48,512]{3,2,1,0:T(8,128)(2,1)} %scene.1) | copy-start | bytes 2359300

commit v4 on v3

--- a/solution.py
+++ b/solution.py
@@ -47,7 +47,7 @@
     held = jnp.zeros((8, 128), jnp.int32)
     count = jnp.zeros((8, 128), jnp.int32)
     for b in range(48):
-        hit = owner == area[b, 0]
+        hit = owner == area[0, b]
         take = jnp.logical_and(hit, count == place)
         source = jnp.where(take, b, source)
         held = jnp.where(take, 1, held)
@@ -56,31 +56,25 @@
     table[1] = held
 
 
-def stage_columns(scene, wide, staged):
-    for part in range(2):
-        for a in range(8):
-            n = part * 8 + a
-            x = scene[part, a].astype(F32)
-            for c in range(4):
-                wide[c, n * 48 : (n + 1) * 48, :] = x[:, c * 128 : (c + 1) * 128]
+def stage_columns(lines, wide, staged):
+    for n in range(16):
+        wide[n * 48 : (n + 1) * 48, :] = lines[n // 8, n % 8].astype(F32)
 
     def row(b, _):
-        for c in range(4):
-            staged[c, b] = wide[c, pl.ds(b, 16, stride=48), :].astype(BF16)
+        staged[b] = wide[pl.ds(b, 16, stride=48), :].astype(BF16)
         return 0
 
-    lax.fori_loop(0, 48, row, 0, unroll=4)
-
-
-def build_own(w, src, weights, z0, lhs):
+    lax.fori_loop(0, 48, row, 0, unroll=8)
+
+
+def build_own(w, src, weights, rows, at, lhs):
     look = (lanes((8, 128)) // 16) % 4
     for r in range(4):
         s = w * 4 + r
         table = weights * (ROWS[r] * src[1, 0, s].astype(F32))
-        own = z0[src[0, 0, s]].astype(F32).reshape(4, 2, 8, 128)
-        tables = [jnp.where(look == l, table, 0.0) for l in range(4)]
-        spread = jnp.stack([own * t[None, None] for t in tables], axis=1)
-        lhs[w, :, r * 128 : (r + 1) * 128] = spread.reshape(256, 128).astype(BF16)
+        own = rows[src[0, 0, s]].astype(F32).reshape(2, 8, 128)
+        spread = jnp.stack([own * jnp.where(look == l, table, 0.0)[None] for l in range(4)], axis=0)
+        lhs[w, pl.ds(at, 64), r * 128 : (r + 1) * 128] = spread.reshape(64, 128).astype(BF16)
 
 
 def window_sums(w, src, weights, z, lhs):
@@ -129,8 +123,8 @@
 
 def pairs_kernel(
     area, scene, recv,
-    wide, staged, table, src, z0, z1, z2, z3, lhs, own_power, res,
-    local_sem, a_send, a_recv, b_send, b_recv, c_send, c_recv,
+    lines, wide, staged, mate, table, src, z0, z1, z2, z3, lhs, own_power, res,
+    local_sem, read_sem, a_send, a_recv, b_send, b_recv, c_send, c_recv,
 ):
     zs = (z0, z1, z2, z3)
     k = lax.axis_index("region")
@@ -147,6 +141,11 @@
     def rows16(start):
         return pl.ds(pl.multiple_of(start, 16), 16)
 
+    reads = {}
+    for j in (2, 3, 0, 1):
+        columns = pl.ds(pl.multiple_of(tile(j) * 128, 128), 128)
+        reads[j] = pltpu.make_async_copy(scene.at[:, :, :, columns], lines.at[j], read_sem.at[j])
+        reads[j].start()
     barrier = pltpu.get_barrier_semaphore()
     for peer in (left, right):
         pl.semaphore_signal(barrier, inc=1, device_id=peer, device_id_type=MESH)
@@ -162,10 +161,9 @@
 
     lax.fori_loop(0, 32, greet, 0)
 
-    sort_rows(area, table)
-    sorted_rows = pltpu.make_async_copy(table, src, local_sem.at[0])
-    sorted_rows.start()
-    stage_columns(scene, wide, staged)
+    for j in (2, 3):
+        reads[j].wait()
+        stage_columns(lines.at[j], wide.at[j], staged.at[j])
     pl.semaphore_wait(barrier, 33)
 
     def remote(from_ref, to_ref, send, recv, peer):
@@ -175,13 +173,18 @@
         )
 
     a_copies = {}
-    for j in (2, 3, 1):
-        to = tile(j)
-        a_copies[j] = remote(
-            staged.at[to], zs[0].at[:, rows16(q * 16), :], a_send.at[j], a_recv.at[j],
-            (k, z * 4 + to),
-        )
-        a_copies[j].start()
+
+    def exchange(n, j, land):
+        peer = (k, z * 4 + tile(j))
+        a_copies[n] = remote(staged.at[j], land, a_send.at[n], a_recv.at[n], peer)
+        a_copies[n].start()
+
+    here16 = z0.at[:, rows16(q * 16), :]
+    exchange(2, 2, here16)
+    exchange(3, 3, here16)
+    for j in (0, 1):
+        reads[j].wait()
+        stage_columns(lines.at[j], wide.at[j], staged.at[j])
 
     def near(j, side):
         return zs[1 + j // 2].at[:, rows16(side * 32 + ((core + j) % 2) * 16), :]
@@ -189,61 +192,88 @@
     b_copies = {}
 
     def send_along(j):
-        data = staged.at[q] if j == 0 else zs[0].at[:, rows16(tile(j) * 16), :]
+        data = staged.at[0] if j == 0 else zs[0].at[:, rows16(tile(j) * 16), :]
         for side, peer in ((0, right), (1, left)):
             n = side * 4 + j
             b_copies[j, side] = remote(data, near(j, side), b_send.at[n], b_recv.at[n], peer)
             b_copies[j, side].start()
 
     send_along(0)
-    own = pltpu.make_async_copy(staged.at[q], zs[0].at[:, rows16(q * 16), :], local_sem.at[1])
+    exchange(1, 1, here16)
+    exchange(0, 1, mate)
+    own = pltpu.make_async_copy(staged.at[0], here16, local_sem.at[1])
     own.start()
-    for j in (1, 2, 3):
+    sort_rows(area, table)
+    sorted_rows = pltpu.make_async_copy(table, src, local_sem.at[0])
+    sorted_rows.start()
+    a_copies[1].wait_recv()
+    send_along(1)
+    a_copies[0].wait_recv()
+    sorted_rows.wait()
+
+    weights = column_weights()
+    q64 = [pl.multiple_of(tile(j) * 64, 64) for j in range(4)]
+
+    def build_near(w, _):
+        build_own(w, src, weights, staged.at[0], q64[0], lhs)
+        build_own(w, src, weights, mate, q64[1], lhs)
+        return 0
+
+    lax.fori_loop(0, 16, build_near, 0, unroll=2)
+    for j in (2, 3):
         a_copies[j].wait_recv()
         send_along(j)
     own.wait()
-    sorted_rows.wait()
-
-    weights = column_weights()
 
     def send_results(o, g):
-        for p in range(4):
-            here = jnp.logical_and(o == k, q == p)
+        for j in (2, 3, 1, 0):
+            p = tile(j)
             block, land = res.at[g, o * 4 + p], recv.at[g, k * 4 + q]
-
-            @pl.when(here)
+            away = remote(block, land, c_send.at[g], c_recv.at[g], (o, z * 4 + p))
+            if j:
+                away.start()
+                continue
+
+            @pl.when(o == k)
             def _():
                 pltpu.make_async_copy(block, land, c_recv.at[g]).start()
 
-            @pl.when(jnp.logical_not(here))
+            @pl.when(o != k)
             def _():
-                remote(block, land, c_send.at[g], c_recv.at[g], (o, z * 4 + p)).start()
+                away.start()
+
+    def z0_tile(j):
+        return z0.at[:, rows16(tile(j) * 16), :]
+
+    def distant(n, u):
+        x = (1 - (n // 2) * (1 - n // 3)) if u == 0 else (n % 2) * (1 - n // 3)
+        y = 2 - (n + 1) // 2 if u == 0 else 2 + (n + 1) // 2
+        return ((k // 4 + x) % 2) * 4 + (k + y) % 4
 
     def group(g):
+        def windows(regions):
+            pairs = [(o, o * 2 + h) for o in regions for h in range(2)]
+            if g == 0:
+                for _, w in pairs:
+                    for j in (2, 3):
+                        build_own(w, src, weights, z0_tile(j), q64[j], lhs)
+            sums = [window_sums(w, src, weights, zs[g], lhs) for _, w in pairs]
+            if g == 0:
+                for (_, w), (_, intensity) in zip(pairs, sums):
+                    own_intensities(w, intensity, own_power)
+            for n, ((o, w), (full, intensity)) in enumerate(zip(pairs, sums)):
+                h = n % 2
+                block = coherence(full, intensity, own_power[w])
+                res[g, pl.ds(o * 4, 4), h * 2 : h * 2 + 2] = block
+                if h:
+                    send_results(o, g)
+
         def step(n, _):
-            regions = (
-                ((k // 4 + n) % 2) * 4 + (k + n + 1) % 4,
-                ((k // 4 + n + 1) % 2) * 4 + (k + n + 3) % 4,
-            )
             if g == 0:
-                for o in regions:
-                    for h in range(2):
-                        build_own(o * 2 + h, src, weights, zs[0], lhs)
-            sums = [
-                window_sums(o * 2 + h, src, weights, zs[g], lhs)
-                for o in regions
-                for h in range(2)
-            ]
-            if g == 0:
-                for m, o in enumerate(regions):
-                    for h in range(2):
-                        own_intensities(o * 2 + h, sums[m * 2 + h][1], own_power)
-            for m, o in enumerate(regions):
-                for h in range(2):
-                    full, intensity = sums[m * 2 + h]
-                    block = coherence(full, intensity, own_power[o * 2 + h])
-                    res[g, pl.ds(o * 4, 4), h * 2 : h * 2 + 2] = block
-                send_results(o, g)
+                windows([distant(n, 0)])
+                windows([distant(n, 1)])
+            else:
+                windows([distant(n, 0), distant(n, 1)])
             return 0
 
         lax.fori_loop(0, 4, step, 0)
@@ -264,13 +294,11 @@
         ))
         relays[-1].start()
 
-    relay(0)
-    relay(1)
-    for j in (2, 3):
-        b_copies[j, 1].wait_recv()
-        relay(j)
     for j in (2, 3):
         b_copies[j, 0].wait_recv()
+        b_copies[j, 1].wait_recv()
+        relay(j - 2)
+        relay(j)
     group(2)
     for copy in relays:
         copy.wait_recv()
@@ -284,9 +312,14 @@
         pltpu.make_async_copy(res.at[g], recv.at[g], c_recv.at[g]).wait()
 
 
-def finish_kernel(recv, out, mixed):
+def finish_kernel(recv, out, got, built, mixed, read_sem, write_sem):
     z = lax.axis_index("acq") // 4
     low = lanes((8, 128)) < 64
+    reads = []
+    for n in range(4):
+        some = pl.ds(n * 8, 8)
+        reads.append(pltpu.make_async_copy(recv.at[:, some], got.at[n], read_sem.at[n]))
+        reads[-1].start()
 
     def arrange(x, y, m):
         def half_turn(v):
@@ -298,38 +331,49 @@
         both = both.transpose(0, 2, 1, 3, 4, 5, 6)
         mixed[m] = both.reshape(1024, 128)
 
-    parts = [recv[g].astype(F32).reshape(2, 4, 2, 4, 8, 128) for g in range(4)]
-    arrange(parts[0], parts[3], 0)
-    near = jnp.concatenate([parts[1][:, 0:2], parts[2][:, 2:4]], axis=1)
-    far = jnp.concatenate([parts[2][:, 0:2], parts[1][:, 2:4]], axis=1)
-    arrange(near, far, 1)
-    for i in range(8):
-        for m in range(2):
-            y = mixed[m, pl.ds(i, 128, stride=8), :].T
-            for n in range(8):
-                if m == 0:
-                    offset, t = (n // 4) * 2, n % 4
-                else:
-                    offset, t = 3 + (n // 2) % 2 * 2, (n // 4) * 2 + n % 2
-                at = ((z + offset) % 4) * 32 + t * 8
-                for part in range(2):
-                    lane = n * 16 + part * 8
-                    out[part, i, pl.ds(pl.multiple_of(at, 8), 8), :] = y[lane : lane + 8]
+    writes = []
+    for n in range(4):
+        reads[n].wait()
+        parts = [got[n, g].astype(F32).reshape(2, 4, 2, 4, 8, 128) for g in range(4)]
+        arrange(parts[0], parts[3], 0)
+        near = jnp.concatenate([parts[1][:, 0:2], parts[2][:, 2:4]], axis=1)
+        far = jnp.concatenate([parts[2][:, 0:2], parts[1][:, 2:4]], axis=1)
+        arrange(near, far, 1)
+        for i in range(8):
+            for m in range(2):
+                y = mixed[m, pl.ds(i, 128, stride=8), :].T
+                for t in range(8):
+                    if m == 0:
+                        offset, tile = (t // 4) * 2, t % 4
+                    else:
+                        offset, tile = 3 + (t // 2) % 2 * 2, (t // 4) * 2 + t % 2
+                    at = pl.multiple_of(((z + offset) % 4) * 32 + tile * 8, 8)
+                    for part in range(2):
+                        lane = t * 16 + part * 8
+                        built[n, part, i, pl.ds(at, 8), :] = y[lane : lane + 8]
+        columns = pl.ds(n * 128, 128)
+        writes.append(
+            pltpu.make_async_copy(built.at[n], out.at[:, :, :, columns], write_sem.at[n])
+        )
+        writes[-1].start()
+    for write in writes:
+        write.wait()
 
 
 def local(scene_lines, assigned_area):
     smem = pl.BlockSpec(memory_space=pltpu.SMEM)
-    vmem = pl.BlockSpec(memory_space=pltpu.VMEM)
-    hbm = pl.BlockSpec(memory_space=pl.ANY)
+    hbm = pl.BlockSpec(memory_space=pltpu.HBM)
     blocks = (4, 32, 4, 16, 128)
     got = pl.pallas_call(
         pairs_kernel,
         out_shape=jax.ShapeDtypeStruct(blocks, BF16),
-        in_specs=[smem, vmem],
+        in_specs=[smem, hbm],
         out_specs=hbm,
         scratch_shapes=[
+            pltpu.VMEM((4, 2, 8, 48, 128), BF16),
             pltpu.VMEM((4, 768, 128), F32),
             pltpu.VMEM((4, 48, 16, 128), BF16),
+            pltpu.VMEM((48, 16, 128), BF16),
             pltpu.VMEM((2, 8, 128), jnp.int32),
             pltpu.SMEM((2, 8, 128), jnp.int32),
             pltpu.VMEM((48, 64, 128), BF16),
@@ -342,23 +386,29 @@
             pltpu.SemaphoreType.DMA((2,)),
             pltpu.SemaphoreType.DMA((4,)),
             pltpu.SemaphoreType.DMA((4,)),
+            pltpu.SemaphoreType.DMA((4,)),
             pltpu.SemaphoreType.DMA((12,)),
             pltpu.SemaphoreType.DMA((12,)),
             pltpu.SemaphoreType.DMA((4,)),
             pltpu.SemaphoreType.DMA((4,)),
         ],
         compiler_params=pltpu.CompilerParams(
-            vmem_limit_bytes=40 << 20, collective_id=0, has_side_effects=True
+            vmem_limit_bytes=61 << 20, collective_id=0, has_side_effects=True
         ),
-    )(assigned_area, scene_lines)
+    )(assigned_area.reshape(1, 48), scene_lines)
     return pl.pallas_call(
         finish_kernel,
-        grid=(4,),
         out_shape=jax.ShapeDtypeStruct((2, 8, 128, 512), F32),
-        in_specs=[pl.BlockSpec((4, 8, 4, 16, 128), lambda n: (0, n, 0, 0, 0))],
-        out_specs=pl.BlockSpec((2, 8, 128, 128), lambda n: (0, 0, 0, n)),
-        scratch_shapes=[pltpu.VMEM((2, 1024, 128), F32)],
-        compiler_params=pltpu.CompilerParams(vmem_limit_bytes=32 << 20),
+        in_specs=[pl.BlockSpec(memory_space=pltpu.HBM)],
+        out_specs=pl.BlockSpec(memory_space=pltpu.HBM),
+        scratch_shapes=[
+            pltpu.VMEM((4, 4, 8, 4, 16, 128), BF16),
+            pltpu.VMEM((4, 2, 8, 128, 128), F32),
+            pltpu.VMEM((2, 1024, 128), F32),
+            pltpu.SemaphoreType.DMA((4,)),
+            pltpu.SemaphoreType.DMA((4,)),
+        ],
+        compiler_params=pltpu.CompilerParams(vmem_limit_bytes=61 << 20),
     )(got)
 
 

time: 56.4 us -> 53.9 us (0.956)
  local copies, waits for them, and re-layouts: 1.87 us -> 0 us
  Pallas kernels: 54.4 us -> 53.7 us
    unnamed x3 -> x0, local copies, waits for them, and re-layouts: 1.87 us -> none
    pallas_call x1, Pallas kernels: 50.7 us -> 49.5 us  [local(): pl.pallas_call(pairs_kernel, out_shape=jax.ShapeDtypeStruct(blocks, BF16)...]
where the time goes in v4:
time: 53.9 us; the launch traced here: 53.7 us
  Pallas kernels  53.7 us (100%)
    pallas_call x1, Pallas kernels, local(): pl.pallas_call(pairs_kernel, out_shape=jax.ShapeDtypeStruct(blocks, BF16)...  49.5 us
    pallas_call x1, Pallas kernels, local(): pl.pallas_call(finish_kernel, out_shape=jax.ShapeDtypeStruct((2, 8, 128,...  4.21 us

profile of v4, /device:TPU:1, one launch (start us, length us, event | category | flops | bytes accessed | tf_op | source)
XLA Modules:
  0.0 53.7 jit_solution(18429390321511689917)
XLA Ops:
  0.0 49.5 %shard_map.28.recv = bf16[4,32,4,16,128]{4,3,2,1,0:T(8,128)(2,1)} custom-call(s32[1,48]{1,0:T(1,128)} %bitcast.1, bf16[2,8,48,512]{3,2,1,0:T(8,128)(2,1)} %scene.1), custom_call_target="tpu_custom_call" | custom-call | tf_op jit(solution)/shard_map/pallas_call | solution.py:367
  49.5 4.2 %shard_map.29 = f32[2,8,128,512]{3,2,1,0:T(8,128)} custom-call(bf16[4,32,4,16,128]{4,3,2,1,0:T(8,128)(2,1)} %shard_map.28.recv), custom_call_target="tpu_custom_call" | custom-call | tf_op jit(solution)/shard_map/pallas_call | solution.py:399

commit v5 on v4

--- a/solution.py
+++ b/solution.py
@@ -121,12 +121,30 @@
     return (total.reshape(4, 4, 8, 128) * scale).reshape(4, 2, 16, 128).astype(BF16)
 
 
+def side_by_side(x, y, mixed):
+    low = lanes((8, 128)) < 64
+
+    def half_turn(v):
+        return pltpu.roll(v.reshape(512, 128), 64, axis=1).reshape(v.shape)
+
+    first = jnp.where(low, x, half_turn(y))
+    second = jnp.where(low, half_turn(x), y)
+    both = jnp.stack([first, second], axis=3)
+    both = both.transpose(0, 2, 1, 3, 4, 5, 6)
+    mixed[...] = both.reshape(1024, 128)
+
+
+def blocks_of(x):
+    return x.astype(F32).reshape(2, 4, 2, 4, 8, 128)
+
+
 def pairs_kernel(
-    area, scene, recv,
-    lines, wide, staged, mate, table, src, z0, z1, z2, z3, lhs, own_power, res,
-    local_sem, read_sem, a_send, a_recv, b_send, b_recv, c_send, c_recv,
+    area, scene, recv, turned,
+    lines, wide, staged, mate, table, src, z0, z1, z2, z3, lhs, own_power, res, landed, mixed, built,
+    turn_sem, local_sem, read_sem, a_send, a_recv, b_send, b_recv, c_send, c_recv,
 ):
     zs = (z0, z1, z2, z3)
+    lands = (recv.at[0], landed.at[0], landed.at[1], recv.at[1])
     k = lax.axis_index("region")
     acq = lax.axis_index("acq")
     z = acq // 4
@@ -228,7 +246,7 @@
     def send_results(o, g):
         for j in (2, 3, 1, 0):
             p = tile(j)
-            block, land = res.at[g, o * 4 + p], recv.at[g, k * 4 + q]
+            block, land = res.at[g, o * 4 + p], lands[g].at[k * 4 + q]
             away = remote(block, land, c_send.at[g], c_recv.at[g], (o, z * 4 + p))
             if j:
                 away.start()
@@ -269,11 +287,7 @@
                     send_results(o, g)
 
         def step(n, _):
-            if g == 0:
-                windows([distant(n, 0)])
-                windows([distant(n, 1)])
-            else:
-                windows([distant(n, 0), distant(n, 1)])
+            windows([distant(n, 0), distant(n, 1)])
             return 0
 
         lax.fori_loop(0, 4, step, 0)
@@ -304,71 +318,91 @@
         copy.wait_recv()
     group(3)
 
+    for g in (1, 2):
+        pltpu.make_async_copy(res.at[g], lands[g], c_recv.at[g]).wait()
+
+    def turn(n, _):
+        same = blocks_of(landed[0, pl.ds(n * 8, 8)])
+        cross = blocks_of(landed[1, pl.ds(n * 8, 8)])
+        near = jnp.concatenate([same[:, 0:2], cross[:, 2:4]], axis=1)
+        far = jnp.concatenate([cross[:, 0:2], same[:, 2:4]], axis=1)
+        side_by_side(near, far, mixed)
+        for i in range(8):
+            y = mixed[pl.ds(i, 128, stride=8), :].T
+            for x in range(2):
+                for side in range(2):
+                    for part in range(2):
+                        lane = x * 64 + side * 32 + part * 8
+                        pair = jnp.concatenate([y[lane : lane + 8], y[lane + 16 : lane + 24]], axis=0)
+                        built[n, part, i, side, x * 16 : x * 16 + 16, :] = pair.astype(BF16)
+        columns = pl.ds(pl.multiple_of(n * 128, 128), 128)
+        pltpu.make_async_copy(
+            built.at[n], turned.at[:, :, :, :, columns], turn_sem.at[n]
+        ).start()
+        return 0
+
+    lax.fori_loop(0, 4, turn, 0)
+
     for copy in list(a_copies.values()) + list(b_copies.values()) + relays:
         copy.wait_send()
+    for n in range(4):
+        columns = pl.ds(n * 128, 128)
+        pltpu.make_async_copy(
+            built.at[n], turned.at[:, :, :, :, columns], turn_sem.at[n]
+        ).wait()
     for g in range(4):
         some = pl.ds(0, 31)
-        pltpu.make_async_copy(res.at[g, some], recv.at[g, some], c_send.at[g]).wait()
-        pltpu.make_async_copy(res.at[g], recv.at[g], c_recv.at[g]).wait()
-
-
-def finish_kernel(recv, out, got, built, mixed, read_sem, write_sem):
+        pltpu.make_async_copy(res.at[g, some], lands[g].at[some], c_send.at[g]).wait()
+    for g in (0, 3):
+        pltpu.make_async_copy(res.at[g], lands[g], c_recv.at[g]).wait()
+
+
+def finish_kernel(recv, turned, out, wide, built, mixed, write_sem, wide_sem):
     z = lax.axis_index("acq") // 4
-    low = lanes((8, 128)) < 64
-    reads = []
+
+    def rows_of(offset):
+        return pl.ds(pl.multiple_of(((z + offset) % 4) * 32, 32), 32)
+
+    copies = []
+
+    def write(from_ref, to_ref, sem):
+        copies.append(pltpu.make_async_copy(from_ref, to_ref, sem))
+        copies[-1].start()
+
+    for part in range(2):
+        wide[part] = turned[part].astype(F32)
+        for d in range(2):
+            land = out.at[part, :, rows_of(3 + 2 * d)]
+            write(wide.at[part, :, d], land, wide_sem.at[part, d])
     for n in range(4):
-        some = pl.ds(n * 8, 8)
-        reads.append(pltpu.make_async_copy(recv.at[:, some], got.at[n], read_sem.at[n]))
-        reads[-1].start()
-
-    def arrange(x, y, m):
-        def half_turn(v):
-            return pltpu.roll(v.reshape(512, 128), 64, axis=1).reshape(v.shape)
-
-        first = jnp.where(low, x, half_turn(y))
-        second = jnp.where(low, half_turn(x), y)
-        both = jnp.stack([first, second], axis=3)
-        both = both.transpose(0, 2, 1, 3, 4, 5, 6)
-        mixed[m] = both.reshape(1024, 128)
-
-    writes = []
-    for n in range(4):
-        reads[n].wait()
-        parts = [got[n, g].astype(F32).reshape(2, 4, 2, 4, 8, 128) for g in range(4)]
-        arrange(parts[0], parts[3], 0)
-        near = jnp.concatenate([parts[1][:, 0:2], parts[2][:, 2:4]], axis=1)
-        far = jnp.concatenate([parts[2][:, 0:2], parts[1][:, 2:4]], axis=1)
-        arrange(near, far, 1)
+        some = slice(n * 8, n * 8 + 8)
+        side_by_side(blocks_of(recv[0, some]), blocks_of(recv[1, some]), mixed)
         for i in range(8):
-            for m in range(2):
-                y = mixed[m, pl.ds(i, 128, stride=8), :].T
-                for t in range(8):
-                    if m == 0:
-                        offset, tile = (t // 4) * 2, t % 4
-                    else:
-                        offset, tile = 3 + (t // 2) % 2 * 2, (t // 4) * 2 + t % 2
-                    at = pl.multiple_of(((z + offset) % 4) * 32 + tile * 8, 8)
-                    for part in range(2):
-                        lane = t * 16 + part * 8
-                        built[n, part, i, pl.ds(at, 8), :] = y[lane : lane + 8]
+            y = mixed[pl.ds(i, 128, stride=8), :].T
+            for t in range(8):
+                for part in range(2):
+                    lane, at = t * 16 + part * 8, (t % 4) * 8
+                    built[n, t // 4, part, i, at : at + 8, :] = y[lane : lane + 8]
         columns = pl.ds(n * 128, 128)
-        writes.append(
-            pltpu.make_async_copy(built.at[n], out.at[:, :, :, columns], write_sem.at[n])
-        )
-        writes[-1].start()
-    for write in writes:
-        write.wait()
+        for d in range(2):
+            write(built.at[n, d], out.at[:, :, rows_of(2 * d), columns], write_sem.at[n, d])
+    for copy in copies:
+        copy.wait()
 
 
 def local(scene_lines, assigned_area):
     smem = pl.BlockSpec(memory_space=pltpu.SMEM)
+    vmem = pl.BlockSpec(memory_space=pltpu.VMEM)
     hbm = pl.BlockSpec(memory_space=pltpu.HBM)
     blocks = (4, 32, 4, 16, 128)
     got = pl.pallas_call(
         pairs_kernel,
-        out_shape=jax.ShapeDtypeStruct(blocks, BF16),
+        out_shape=[
+            jax.ShapeDtypeStruct((2, 32, 4, 16, 128), BF16),
+            jax.ShapeDtypeStruct((2, 8, 2, 32, 512), BF16),
+        ],
         in_specs=[smem, hbm],
-        out_specs=hbm,
+        out_specs=[hbm, hbm],
         scratch_shapes=[
             pltpu.VMEM((4, 2, 8, 48, 128), BF16),
             pltpu.VMEM((4, 768, 128), F32),
@@ -383,6 +417,10 @@
             pltpu.VMEM((16, 256, 512), BF16),
             pltpu.VMEM((16, 16, 8, 128), F32),
             pltpu.VMEM(blocks, BF16),
+            pltpu.VMEM((2, 32, 4, 16, 128), BF16),
+            pltpu.VMEM((1024, 128), F32),
+            pltpu.VMEM((4, 2, 8, 2, 32, 128), BF16),
+            pltpu.SemaphoreType.DMA((4,)),
             pltpu.SemaphoreType.DMA((2,)),
             pltpu.SemaphoreType.DMA((4,)),
             pltpu.SemaphoreType.DMA((4,)),
@@ -393,23 +431,26 @@
             pltpu.SemaphoreType.DMA((4,)),
         ],
         compiler_params=pltpu.CompilerParams(
-            vmem_limit_bytes=61 << 20, collective_id=0, has_side_effects=True
+            vmem_limit_bytes=40 << 20, collective_id=0, has_side_effects=True
         ),
-    )(assigned_area.reshape(1, 48), scene_lines)
+    )(
+        pltpu.with_memory_space_constraint(assigned_area.reshape(1, 48), pltpu.HBM),
+        pltpu.with_memory_space_constraint(scene_lines, pltpu.HBM),
+    )
     return pl.pallas_call(
         finish_kernel,
         out_shape=jax.ShapeDtypeStruct((2, 8, 128, 512), F32),
-        in_specs=[pl.BlockSpec(memory_space=pltpu.HBM)],
-        out_specs=pl.BlockSpec(memory_space=pltpu.HBM),
+        in_specs=[vmem, vmem],
+        out_specs=hbm,
         scratch_shapes=[
-            pltpu.VMEM((4, 4, 8, 4, 16, 128), BF16),
-            pltpu.VMEM((4, 2, 8, 128, 128), F32),
-            pltpu.VMEM((2, 1024, 128), F32),
-            pltpu.SemaphoreType.DMA((4,)),
-            pltpu.SemaphoreType.DMA((4,)),
+            pltpu.VMEM((2, 8, 2, 32, 512), F32),
+            pltpu.VMEM((4, 2, 2, 8, 32, 128), F32),
+            pltpu.VMEM((1024, 128), F32),
+            pltpu.SemaphoreType.DMA((4, 2)),
+            pltpu.SemaphoreType.DMA((2, 2)),
         ],
-        compiler_params=pltpu.CompilerParams(vmem_limit_bytes=61 << 20),
-    )(got)
+        compiler_params=pltpu.CompilerParams(vmem_limit_bytes=32 << 20),
+    )(*got)
 
 
 def solution(mesh):

time: 53.9 us -> 52.2 us (0.968)
  Pallas kernels: 53.7 us -> 52.1 us
    pallas_call x1, Pallas kernels: 4.21 us -> 2.43 us  [local(): pl.pallas_call(finish_kernel, out_shape=jax.ShapeDtypeStruct((2, 8, 128,...]
where the time goes in v5:
time: 52.2 us; the launch traced here: 52.1 us
  Pallas kernels  52.1 us (100%)
    pallas_call x1, Pallas kernels, local(): pl.pallas_call(pairs_kernel, out_shape=[jax.ShapeDtypeStruct((2, 32, 4, 1...  49.6 us
    pallas_call x1, Pallas kernels, local(): pl.pallas_call(finish_kernel, out_shape=jax.ShapeDtypeStruct((2, 8, 128,...  2.43 us

profile of v5, /device:TPU:1, one launch (start us, length us, event | category | flops | bytes accessed | tf_op | source)
XLA Modules:
  0.0 52.1 jit_solution(12675863197954763686)
XLA Ops:
  0.0 49.6 %shard_map.28 = (bf16[2,32,4,16,128]{4,3,2,1,0:T(8,128)(2,1)S(1)}, bf16[2,8,2,32,512]{4,3,2,1,0:T(8,128)(2,1)S(1)}) custom-call(s32[1,48]{1,0:T(1,128)} %bitcast.1, bf16[2,8,48,512]{3,2,1,0:T(8,128)(2,1)} %scene.1), custom_call_target="tpu_custom_call" | custom-call | tf_op jit(solution)/shard_map/pallas_call | solution.py:398
  49.6 2.4 %shard_map.29 = f32[2,8,128,512]{3,2,1,0:T(8,128)} custom-call(bf16[2,32,4,16,128]{4,3,2,1,0:T(8,128)(2,1)S(1)} %get-tuple-element.7.recv, bf16[2,8,2,32,512]{4,3,2,1,0:T(8,128)(2,1)S(1)} %get-tuple-element.8.turned), custom_call_target="tpu_custom_call" | custom-call | tf_op jit(solution)/shard_map/pallas_call | solution.py:440

commit v6 on v5

--- a/solution.py
+++ b/solution.py
@@ -101,13 +101,23 @@
 
 
 def own_intensities(w, intensity, own_power):
-    turned = intensity.T
-    low = lanes((8, 128)) < 64
+    lane = lanes((8, 128))
+    same = lane % 16 == lax.broadcasted_iota(jnp.int32, (8, 128), 0)
+    picked = []
     for q in range(4):
+        mine = jnp.logical_and(same, (lane // 16) % 4 == q)
         for l in range(4):
-            first = jnp.broadcast_to(turned[q * 16 : q * 16 + 8, l : l + 1], (8, 128))
-            second = jnp.broadcast_to(turned[64 + q * 16 : 72 + q * 16, l : l + 1], (8, 128))
-            own_power[w, q * 4 + l] = jnp.where(low, first, second)
+            row = jnp.broadcast_to(intensity[l : l + 1], (8, 128))
+            picked.append(jnp.where(mine, row, 0.0))
+    picked = jnp.concatenate(picked, axis=0)
+    coarse = picked.astype(BF16)
+    fine = (picked - coarse.astype(F32)).astype(BF16)
+    terms = jnp.concatenate([coarse, fine], axis=1)
+    lane = lanes((128, 256)) % 128
+    half = lax.broadcasted_iota(jnp.int32, (128, 256), 0)
+    spread = jnp.where((lane < 64) == (half < 64), 1.0, 0.0).astype(BF16)
+    both = lax.dot_general(terms, spread, NT, preferred_element_type=F32)
+    own_power[w] = both.reshape(16, 8, 128)
 
 
 def coherence(full, intensity, own):

time: 52.2 us -> 50.8 us (0.973)
  Pallas kernels: 52.1 us -> 50.7 us
    pallas_call x1, Pallas kernels: 49.6 us -> 48.3 us  [local(): pl.pallas_call(pairs_kernel, out_shape=[jax.ShapeDtypeStruct((2, 32, 4, 1...]
where the time goes in v6:
time: 50.8 us; the launch traced here: 50.7 us
  Pallas kernels  50.7 us (100%)
    pallas_call x1, Pallas kernels, local(): pl.pallas_call(pairs_kernel, out_shape=[jax.ShapeDtypeStruct((2, 32, 4, 1...  48.3 us
    pallas_call x1, Pallas kernels, local(): pl.pallas_call(finish_kernel, out_shape=jax.ShapeDtypeStruct((2, 8, 128,...  2.43 us

profile of v6, /device:TPU:1, one launch (start us, length us, event | category | flops | bytes accessed | tf_op | source)
XLA Modules:
  0.0 50.7 jit_solution(10060479053387839869)
XLA Ops:
  0.0 48.3 %shard_map.28 = (bf16[2,32,4,16,128]{4,3,2,1,0:T(8,128)(2,1)S(1)}, bf16[2,8,2,32,512]{4,3,2,1,0:T(8,128)(2,1)S(1)}) custom-call(s32[1,48]{1,0:T(1,128)} %bitcast.1, bf16[2,8,48,512]{3,2,1,0:T(8,128)(2,1)} %scene.1), custom_call_target="tpu_custom_call" | custom-call | tf_op jit(solution)/shard_map/pallas_call | solution.py:408
  48.3 2.4 %shard_map.29 = f32[2,8,128,512]{3,2,1,0:T(8,128)} custom-call(bf16[2,32,4,16,128]{4,3,2,1,0:T(8,128)(2,1)S(1)} %get-tuple-element.7.recv, bf16[2,8,2,32,512]{4,3,2,1,0:T(8,128)(2,1)S(1)} %get-tuple-element.8.turned), custom_call_target="tpu_custom_call" | custom-call | tf_op jit(solution)/shard_map/pallas_call | solution.py:450

commit v7 on v6

--- a/solution.py
+++ b/solution.py
@@ -178,16 +178,10 @@
     for peer in (left, right):
         pl.semaphore_signal(barrier, inc=1, device_id=peer, device_id_type=MESH)
 
-    def greet(n, _):
-        o, p = n // 4, n % 4
-
-        @pl.when(jnp.logical_or(o != k, p != q))
-        def _():
-            pl.semaphore_signal(barrier, inc=1, device_id=(o, z * 4 + p), device_id_type=MESH)
-
-        return 0
-
-    lax.fori_loop(0, 32, greet, 0)
+    for n in range(1, 32):
+        o = ((k // 4 + n // 16) % 2) * 4 + (k + n // 4) % 4
+        peer = (o, z * 4 + tile(n % 4))
+        pl.semaphore_signal(barrier, inc=1, device_id=peer, device_id_type=MESH)
 
     for j in (2, 3):
         reads[j].wait()
@@ -248,6 +242,16 @@
         return 0
 
     lax.fori_loop(0, 16, build_near, 0, unroll=2)
+    relays = []
+
+    def relay(j):
+        side, peer = ((0, right), (1, left), (0, right), (1, left))[j]
+        n = 8 + j
+        relays.append(remote(
+            near(j, side), zs[3].at[:, rows16(tile(j) * 16), :], b_send.at[n], b_recv.at[n], peer
+        ))
+        relays[-1].start()
+
     for j in (2, 3):
         a_copies[j].wait_recv()
         send_along(j)
@@ -306,22 +310,13 @@
     for j in (0, 1):
         for side in range(2):
             b_copies[j, side].wait_recv()
+    relay(0)
+    relay(1)
     group(1)
-
-    relays = []
-
-    def relay(j):
-        side, peer = ((0, right), (0, right), (1, left), (1, left))[j]
-        n = 8 + j
-        relays.append(remote(
-            near(j, side), zs[3].at[:, rows16(tile(j) * 16), :], b_send.at[n], b_recv.at[n], peer
-        ))
-        relays[-1].start()
 
     for j in (2, 3):
         b_copies[j, 0].wait_recv()
         b_copies[j, 1].wait_recv()
-        relay(j - 2)
         relay(j)
     group(2)
     for copy in relays:

time: 50.8 us -> 49.4 us (0.972)
  Pallas kernels: 50.7 us -> 49.3 us
    pallas_call x1, Pallas kernels: 48.3 us -> 46.9 us  [local(): pl.pallas_call(pairs_kernel, out_shape=[jax.ShapeDtypeStruct((2, 32, 4, 1...]
where the time goes in v7:
time: 49.4 us; the launch traced here: 49.3 us
  Pallas kernels  49.3 us (100%)
    pallas_call x1, Pallas kernels, local(): pl.pallas_call(pairs_kernel, out_shape=[jax.ShapeDtypeStruct((2, 32, 4, 1...  46.9 us
    pallas_call x1, Pallas kernels, local(): pl.pallas_call(finish_kernel, out_shape=jax.ShapeDtypeStruct((2, 8, 128,...  2.43 us

profile of v7, /device:TPU:1, one launch (start us, length us, event | category | flops | bytes accessed | tf_op | source)
XLA Modules:
  0.0 49.3 jit_solution(13913662504324951872)
XLA Ops:
  0.0 46.9 %shard_map.28 = (bf16[2,32,4,16,128]{4,3,2,1,0:T(8,128)(2,1)S(1)}, bf16[2,8,2,32,512]{4,3,2,1,0:T(8,128)(2,1)S(1)}) custom-call(s32[1,48]{1,0:T(1,128)} %bitcast.1, bf16[2,8,48,512]{3,2,1,0:T(8,128)(2,1)} %scene.1), custom_call_target="tpu_custom_call" | custom-call | tf_op jit(solution)/shard_map/pallas_call | solution.py:403
  46.9 2.4 %shard_map.29 = f32[2,8,128,512]{3,2,1,0:T(8,128)} custom-call(bf16[2,32,4,16,128]{4,3,2,1,0:T(8,128)(2,1)S(1)} %get-tuple-element.7.recv, bf16[2,8,2,32,512]{4,3,2,1,0:T(8,128)(2,1)S(1)} %get-tuple-element.8.turned), custom_call_target="tpu_custom_call" | custom-call | tf_op jit(solution)/shard_map/pallas_call | solution.py:445

commit v8 on v7

--- a/solution.py
+++ b/solution.py
@@ -315,9 +315,10 @@
     group(1)
 
     for j in (2, 3):
-        b_copies[j, 0].wait_recv()
-        b_copies[j, 1].wait_recv()
+        b_copies[j, j - 2].wait_recv()
         relay(j)
+    for j in (2, 3):
+        b_copies[j, 3 - j].wait_recv()
     group(2)
     for copy in relays:
         copy.wait_recv()
@@ -339,7 +340,7 @@
                     for part in range(2):
                         lane = x * 64 + side * 32 + part * 8
                         pair = jnp.concatenate([y[lane : lane + 8], y[lane + 16 : lane + 24]], axis=0)
-                        built[n, part, i, side, x * 16 : x * 16 + 16, :] = pair.astype(BF16)
+                        built[n, part, i, side, x * 16 : x * 16 + 16, :] = pair
         columns = pl.ds(pl.multiple_of(n * 128, 128), 128)
         pltpu.make_async_copy(
             built.at[n], turned.at[:, :, :, :, columns], turn_sem.at[n]
@@ -362,7 +363,7 @@
         pltpu.make_async_copy(res.at[g], lands[g], c_recv.at[g]).wait()
 
 
-def finish_kernel(recv, turned, out, wide, built, mixed, write_sem, wide_sem):
+def finish_kernel(recv, turned, out, built, mixed, write_sem, wide_sem):
     z = lax.axis_index("acq") // 4
 
     def rows_of(offset):
@@ -375,10 +376,9 @@
         copies[-1].start()
 
     for part in range(2):
-        wide[part] = turned[part].astype(F32)
         for d in range(2):
             land = out.at[part, :, rows_of(3 + 2 * d)]
-            write(wide.at[part, :, d], land, wide_sem.at[part, d])
+            write(turned.at[part, :, d], land, wide_sem.at[part, d])
     for n in range(4):
         some = slice(n * 8, n * 8 + 8)
         side_by_side(blocks_of(recv[0, some]), blocks_of(recv[1, some]), mixed)
@@ -404,7 +404,7 @@
         pairs_kernel,
         out_shape=[
             jax.ShapeDtypeStruct((2, 32, 4, 16, 128), BF16),
-            jax.ShapeDtypeStruct((2, 8, 2, 32, 512), BF16),
+            jax.ShapeDtypeStruct((2, 8, 2, 32, 512), F32),
         ],
         in_specs=[smem, hbm],
         out_specs=[hbm, hbm],
@@ -424,7 +424,7 @@
             pltpu.VMEM(blocks, BF16),
             pltpu.VMEM((2, 32, 4, 16, 128), BF16),
             pltpu.VMEM((1024, 128), F32),
-            pltpu.VMEM((4, 2, 8, 2, 32, 128), BF16),
+            pltpu.VMEM((4, 2, 8, 2, 32, 128), F32),
             pltpu.SemaphoreType.DMA((4,)),
             pltpu.SemaphoreType.DMA((2,)),
             pltpu.SemaphoreType.DMA((4,)),
@@ -448,7 +448,6 @@
         in_specs=[vmem, vmem],
         out_specs=hbm,
         scratch_shapes=[
-            pltpu.VMEM((2, 8, 2, 32, 512), F32),
             pltpu.VMEM((4, 2, 2, 8, 32, 128), F32),
             pltpu.VMEM((1024, 128), F32),
             pltpu.SemaphoreType.DMA((4, 2)),

time: 49.4 us -> 49.2 us (level)
  no operation moved by 1% of the time
where the time goes in v8:
time: 49.2 us; the launch traced here: 49.1 us
  Pallas kernels  49.1 us (100%)
    pallas_call x1, Pallas kernels, local(): pl.pallas_call(pairs_kernel, out_shape=[jax.ShapeDtypeStruct((2, 32, 4, 1...  46.9 us
    pallas_call x1, Pallas kernels, local(): pl.pallas_call(finish_kernel, out_shape=jax.ShapeDtypeStruct((2, 8, 128,...  2.23 us

profile of v8, /device:TPU:1, one launch (start us, length us, event | category | flops | bytes accessed | tf_op | source)
XLA Modules:
  0.0 49.1 jit_solution(4328194549908773273)
XLA Ops:
  0.0 46.9 %shard_map.28 = (bf16[2,32,4,16,128]{4,3,2,1,0:T(8,128)(2,1)S(1)}, f32[2,8,2,32,512]{4,3,2,1,0:T(8,128)S(1)}) custom-call(s32[1,48]{1,0:T(1,128)} %bitcast.1, bf16[2,8,48,512]{3,2,1,0:T(8,128)(2,1)} %scene.1), custom_call_target="tpu_custom_call" | custom-call | tf_op jit(solution)/shard_map/pallas_call | solution.py:403
  46.9 2.2 %shard_map.29 = f32[2,8,128,512]{3,2,1,0:T(8,128)} custom-call(bf16[2,32,4,16,128]{4,3,2,1,0:T(8,128)(2,1)S(1)} %get-tuple-element.7.recv, f32[2,8,2,32,512]{4,3,2,1,0:T(8,128)S(1)} %get-tuple-element.8.turned), custom_call_target="tpu_custom_call" | custom-call | tf_op jit(solution)/shard_map/pallas_call | solution.py:445

commit v9 on v8

--- a/solution.py
+++ b/solution.py
@@ -169,20 +169,20 @@
     def rows16(start):
         return pl.ds(pl.multiple_of(start, 16), 16)
 
+    barrier = pltpu.get_barrier_semaphore()
+    for peer in (left, right):
+        pl.semaphore_signal(barrier, inc=1, device_id=peer, device_id_type=MESH)
+
+    for n in range(1, 32):
+        o = ((k // 4 + n // 16) % 2) * 4 + (k + n // 4) % 4
+        peer = (o, z * 4 + tile(n % 4))
+        pl.semaphore_signal(barrier, inc=1, device_id=peer, device_id_type=MESH)
+
     reads = {}
     for j in (2, 3, 0, 1):
         columns = pl.ds(pl.multiple_of(tile(j) * 128, 128), 128)
         reads[j] = pltpu.make_async_copy(scene.at[:, :, :, columns], lines.at[j], read_sem.at[j])
         reads[j].start()
-    barrier = pltpu.get_barrier_semaphore()
-    for peer in (left, right):
-        pl.semaphore_signal(barrier, inc=1, device_id=peer, device_id_type=MESH)
-
-    for n in range(1, 32):
-        o = ((k // 4 + n // 16) % 2) * 4 + (k + n // 4) % 4
-        peer = (o, z * 4 + tile(n % 4))
-        pl.semaphore_signal(barrier, inc=1, device_id=peer, device_id_type=MESH)
-
     for j in (2, 3):
         reads[j].wait()
         stage_columns(lines.at[j], wide.at[j], staged.at[j])

time: 49.2 us -> 49.2 us (level)
  no operation moved by 1% of the time
where the time goes in v9:
time: 49.2 us; the launch traced here: 49.1 us
  Pallas kernels  49.1 us (100%)
    pallas_call x1, Pallas kernels, local(): pl.pallas_call(pairs_kernel, out_shape=[jax.ShapeDtypeStruct((2, 32, 4, 1...  46.9 us
    pallas_call x1, Pallas kernels, local(): pl.pallas_call(finish_kernel, out_shape=jax.ShapeDtypeStruct((2, 8, 128,...  2.23 us

profile of v9, /device:TPU:1, one launch (start us, length us, event | category | flops | bytes accessed | tf_op | source)
XLA Modules:
  0.0 49.1 jit_solution(9136763170189647355)
XLA Ops:
  0.0 46.9 %shard_map.28 = (bf16[2,32,4,16,128]{4,3,2,1,0:T(8,128)(2,1)S(1)}, f32[2,8,2,32,512]{4,3,2,1,0:T(8,128)S(1)}) custom-call(s32[1,48]{1,0:T(1,128)} %bitcast.1, bf16[2,8,48,512]{3,2,1,0:T(8,128)(2,1)} %scene.1), custom_call_target="tpu_custom_call" | custom-call | tf_op jit(solution)/shard_map/pallas_call | solution.py:403
  46.9 2.2 %shard_map.29 = f32[2,8,128,512]{3,2,1,0:T(8,128)} custom-call(bf16[2,32,4,16,128]{4,3,2,1,0:T(8,128)(2,1)S(1)} %get-tuple-element.7.recv, f32[2,8,2,32,512]{4,3,2,1,0:T(8,128)S(1)} %get-tuple-element.8.turned), custom_call_target="tpu_custom_call" | custom-call | tf_op jit(solution)/shard_map/pallas_call | solution.py:445
